TPU v7x, 256 devices: a whole 4x4x8 slice. The times are simulated.
256 devices in a mesh: dyn: 16 (over x_lo, z), phys: 16 (over x_hi, y, core).
Axes of the slice: x: 4 (x_hi: 2, x_lo: 2; x = x_hi * 2 + x_lo), y: 4, z: 8, core: 2. Of those that a mesh axis runs over, the one named last changes fastest.
Arguments:
- initial_state: float32 [72, 256, 2048], P(None, ('dyn', 'phys')), may hold values from -6 to 6
- prev_tendency: float32 [72, 256, 2048], P(None, ('dyn', 'phys')), may hold values from -3 to 3
- analysis: float32 [72, 2, 256, 256], P(None, None, ('dyn', 'phys')), may hold values from -4 to 4
- legendre: float32 [256, 16, 16, 256], P('dyn', None, 'phys'), may hold values from -6 to 6
- nudge_rate: float32 [72], replicated, may hold values from 0.1 to 2
- band_waves: int32 [256], replicated, may hold values from 0 to 255, each once
- cloudy_count: int32 [4096], P(('dyn', 'phys')), may hold values from 1 to 128, as said below
- expert_of: int32 [4096, 1], P(('dyn', 'phys')), may hold values from 0 to 15, as said below
- w_in: bfloat16 [16, 72, 1024], P('phys'), may hold values from -0.75 to 0.75
- w_mid: bfloat16 [16, 1024, 1024], P('phys'), may hold values from -0.1875 to 0.1875
- w_out: bfloat16 [16, 72, 1024], P('phys'), may hold values from -0.1875 to 0.1875
Outputs:
- final_state: float32 [72, 256, 2048], P(None, ('dyn', 'phys'))
- tendency: bfloat16 [72, 256, 2048], P(None, ('dyn', 'phys'))
Inputs may be any that keep to these rules, and one draw needn't show every extreme that they name: `band_waves`: each zonal wavenumber 0 .. 255 stands in exactly one slot. `cloudy_count`: some block of every device has 128 cloudy columns. `expert_of`: among the 16 blocks of one device no network is named more than 2 times; in every group of devices along phys one network is named exactly 2 times by each device of the group.
All inputs are finite; a program needn't handle non-finite values.
Results may differ from a plain program's by a relative error of at most 0.0065.
Values may be sent and summed in bfloat16 or wider, within the bound.
No kernel may reach another device: no remote copies, remote signals or barrier semaphores. Data moves between devices by JAX's collectives and lax.ppermute only.
A program may use at most 128 MiB of HBM per device.

v0:
```python
import math

import jax
import jax.numpy as jnp
import numpy as np
from jax import lax
from jax.sharding import PartitionSpec as P

NB_ROW = 16
CMAX = 128
TIME_STEP = 0.5
HIGH = lax.Precision.HIGH
BOTH = ("dyn", "phys")


def wave_table(waves, n_lon):
    phases = np.arange(waves)[:, None] * np.arange(n_lon)[None, :] % n_lon
    angles = phases.astype(np.float64) * (2.0 * math.pi / n_lon)
    return np.stack([np.cos(angles), -np.sin(angles)], axis=0).astype(np.float32)


def routing(expert_of, n_phys, capacity):
    experts = expert_of[:, 0]
    blocks = experts.shape[0]
    block_order = jnp.arange(blocks, dtype=jnp.int32)
    earlier = (experts[:, None] == experts[None, :]) & (block_order[None, :] < block_order[:, None])
    rank_within = jnp.sum(earlier.astype(jnp.int32), axis=1)
    target = experts * capacity + rank_within
    slots = jnp.arange(n_phys * capacity, dtype=jnp.int32)
    return (target[:, None] == slots[None, :]).astype(jnp.bfloat16)


def physics_local(initial_state, cloudy_count, expert_of, w_in, w_mid, w_out):
    levels, lat_rows, n_lon = initial_state.shape
    n_phys = lax.axis_size("phys")
    blocks = expert_of.shape[0]
    capacity = 2
    columns = initial_state.reshape(levels, blocks, n_lon // NB_ROW).astype(jnp.bfloat16)
    placing = routing(expert_of, n_phys, capacity)
    outgoing = jnp.einsum("bd,lbc->dlc", placing, columns, preferred_element_type=jnp.float32)
    outgoing = outgoing.astype(jnp.bfloat16).reshape(n_phys, capacity, levels, CMAX)
    arrived = lax.all_to_all(outgoing, "phys", split_axis=0, concat_axis=0, tiled=True)
    hidden_one = jax.nn.silu(
        jnp.einsum("qilc,lh->qihc", arrived, w_in[0], preferred_element_type=jnp.float32)
    ).astype(jnp.bfloat16)
    hidden_two = jax.nn.silu(
        jnp.einsum("qihc,hg->qigc", hidden_one, w_mid[0], preferred_element_type=jnp.float32)
    ).astype(jnp.bfloat16)
    computed = jnp.einsum(
        "qigc,lg->qilc", hidden_two, w_out[0], preferred_element_type=jnp.float32
    ).astype(jnp.bfloat16)
    returned = lax.all_to_all(computed, "phys", split_axis=0, concat_axis=0, tiled=True).reshape(
        n_phys * capacity, levels, CMAX
    )
    gathered = jnp.einsum("bd,dlc->lbc", placing, returned, preferred_element_type=jnp.float32)
    cloudy_mask = jnp.arange(CMAX, dtype=jnp.int32)[None, None, :] < cloudy_count[None, :, None]
    masked = jnp.where(cloudy_mask, gathered, 0.0).astype(jnp.bfloat16)
    return masked.reshape(levels, lat_rows, n_lon)


def on_device(
    initial_state,
    prev_tendency,
    analysis,
    legendre,
    nudge_rate,
    band_waves,
    cloudy_count,
    expert_of,
    w_in,
    w_mid,
    w_out,
):
    levels, _, n_lon = initial_state.shape
    waves = band_waves.shape[0]
    coeffs = legendre.shape[3]
    lats = waves
    table = jnp.asarray(wave_table(waves, n_lon))
    wave_ids = jnp.arange(waves, dtype=jnp.int32)
    slot_of = (band_waves[:, None] == wave_ids[None, :]).astype(jnp.bfloat16)
    me = lax.axis_index("dyn") * lax.axis_size("phys") + lax.axis_index("phys")
    own_wave = lax.dynamic_index_in_dim(band_waves, me, 0, keepdims=False)

    def to_slots(field):
        natural = jnp.einsum("lx,rmx->rml", field, table, precision=HIGH) * (1.0 / math.sqrt(n_lon))
        return jnp.einsum(
            "sm,rml->srl", slot_of, natural.astype(jnp.bfloat16), preferred_element_type=jnp.float32
        ).astype(jnp.bfloat16)

    tendency = physics_local(initial_state, cloudy_count, expert_of, w_in, w_mid, w_out)
    first = to_slots(initial_state[:, 0] + TIME_STEP * prev_tendency[:, 0])
    second = to_slots(TIME_STEP * tendency[:, 0].astype(jnp.float32))
    sent = jnp.concatenate([first, second], axis=1)
    got = lax.all_to_all(sent, BOTH, split_axis=0, concat_axis=0, tiled=True)
    got = got.reshape(lats, 2, 2, levels).astype(jnp.float32)

    own_table = lax.all_to_all(
        legendre.astype(jnp.bfloat16), "phys", split_axis=0, concat_axis=2, tiled=True
    ).reshape(lats, coeffs).astype(jnp.float32)

    total_wave = (own_wave + jnp.arange(coeffs, dtype=jnp.int32)).astype(jnp.float32)
    damping = total_wave * (total_wave + 1.0) / (waves * (waves + 1.0))
    rate = nudge_rate[:, None]
    inverse = 1.0 / (1.0 + TIME_STEP * (damping[None, :] + rate))
    pulled = TIME_STEP * rate[None] * analysis[:, :, 0].transpose(1, 0, 2)

    def step(fourier):
        spectral = jnp.einsum("qrl,qk->rlk", fourier, own_table, precision=HIGH) * (
            1.0 / math.sqrt(lats)
        )
        solved = (spectral + pulled) * inverse[None]
        return jnp.einsum("rlk,qk->qrl", solved, own_table, precision=HIGH) * (
            1.0 / math.sqrt(coeffs)
        )

    again = (n_lon / 2.0) / math.sqrt(waves) / math.sqrt(n_lon)
    zero_wave = own_wave == 0
    regain = jnp.stack([jnp.where(zero_wave, 2.0 * again, again), jnp.where(zero_wave, 0.0, again)])
    back = step(got[:, 0])
    back = step(regain[None, :, None] * back + got[:, 1])
    home = lax.all_to_all(back.astype(jnp.bfloat16), BOTH, split_axis=0, concat_axis=0, tiled=True)
    natural = jnp.einsum("sm,srl->rml", slot_of, home, preferred_element_type=jnp.float32)
    final = jnp.einsum("rml,rmx->lx", natural, table, precision=HIGH) * (1.0 / math.sqrt(waves))
    return (final[:, None, :], tendency)


def solution(mesh):
    in_specs = (
        P(None, ("dyn", "phys"), None),
        P(None, ("dyn", "phys"), None),
        P(None, None, ("dyn", "phys"), None),
        P("dyn", None, "phys", None),
        P(),
        P(),
        P(("dyn", "phys")),
        P(("dyn", "phys"), None),
        P("phys", None, None),
        P("phys", None, None),
        P("phys", None, None),
    )
    out_specs = (P(None, ("dyn", "phys"), None), P(None, ("dyn", "phys"), None))
    return jax.shard_map(
        on_device, mesh=mesh, in_specs=in_specs, out_specs=out_specs, check_vma=False
    )
```

profile of v0, /device:TPU:1, one launch (start us, length us, event | category | flops | bytes accessed | tf_op | source)
XLA Modules:
  0.0 137.6 jit_solution(11288121981416905189)
XLA Ops:
  0.6 0.0 copy-start
  0.6 0.0 copy-start.4
  0.7 0.0 copy-start.3
  0.7 0.0 copy-start.9
  0.7 1.0 convert_reduce_fusion.1
  1.7 0.7 fusion.50
  2.3 0.0 copy-start.6
  2.3 2.6 %convert_reduce_fusion = bf16[72,2048]{1,0:T(8,128)(2,1)S(1)} fusion(f32[72,1,2048]{2,1,0:T(1,128)} %param.12), kind=kLoop, calls=%fused_computation.44 | loop fusion | flops 147456 | bytes 884736 | tf_op jit(solution)/shard_map/convert_element_type | solution.py:38
  5.0 0.4 convolution_convert_fusion
  5.4 0.0 copy-done.6
  5.4 1.0 copy.45
  6.5 8.4 %all-to-all-start = ((bf16[16,2,72,128]{3,2,1,0:T(8,128)(2,1)}), bf16[16,2,72,128]{3,2,1,0:T(8,128)(2,1)S(1)}, u32[]{:S(2)}, u32[]{:S(2)}) async-start(bf16[16,2,72,128]{3,2,1,0:T(8,128)(2,1)} %copy.45), calls=%async_computation | async-start | bytes 1179648 | tf_op jit(solution)/shard_map/all_to_all | solution.py:42
  14.9 1.3 dynamic_slice.4
  16.9 2.0 %multiply_add_fusion = f32[72,1,2048]{2,1,0:T(1,128)S(1)} fusion(f32[72,1,2048]{2,1,0:T(1,128)} %param.12, f32[72,1,2048]{2,1,0:T(1,128)} %param.13), kind=kLoop, calls=%fused_computation.45 | loop fusion | flops 294912 | bytes 1769472 | tf_op jit(solution)/shard_map/add | solution.py:91
  18.9 4.3 %fusion.29 = bf16[72,2,256]{2,0,1:T(8,128)(2,1)S(1)} fusion(f32[2,256,2048]{2,1,0:T(8,128)} %constant.45.clone, f32[72,1,2048]{2,1,0:T(1,128)S(1)} %multiply_add_fusion), kind=kOutput, calls=%fused_computation.38 | convolution fusion | flops 453058560 | bytes 4857856 | tf_op jit(solution)/shard_map/lx,rmx->rml/dot_general | solution.py:85
  23.1 0.0 copy-done.4
  23.1 0.3 fusion.35
  23.4 0.6 convert_element_type.71
  24.1 0.0 copy-done.3
  24.1 0.7 copy.74
  24.7 0.0 copy-start.10
  24.7 2.2 %all-to-all-done = bf16[16,2,72,128]{3,2,1,0:T(8,128)(2,1)S(1)} async-done(((bf16[16,2,72,128]{3,2,1,0:T(8,128)(2,1)}), bf16[16,2,72,128]{3,2,1,0:T(8,128)(2,1)S(1)}, u32[]{:S(2)}, u32[]{:S(2)}) %all-to-all-start) | async-done | bytes 589856 | tf_op jit(solution)/shard_map/all_to_all | solution.py:42
  26.9 0.0 copy-done.9
  26.9 6.9 %fusion.6 = bf16[16,2,1024,128]{2,3,1,0:T(8,128)(2,1)} fusion(bf16[16,2,72,128]{3,2,1,0:T(8,128)(2,1)S(1)} %all-to-all-done, bf16[1,72,1024]{2,1,0:T(8,128)(2,1)S(1)} %copy-done.9), kind=kOutput, calls=%fused_computation.10 | convolution fusion | flops 624951296 | bytes 9125888 | tf_op jit(solution)/shard_map/qilc,lh->qihc/dot_general | solution.py:44
  33.8 0.0 copy-done
  33.8 0.0 copy-done.10
  33.9 0.0 copy-start.7
  33.9 16.1 %fusion.17 = bf16[16,2,72,128]{3,2,1,0:T(8,128)(2,1)} fusion(bf16[16,2,1024,128]{2,3,1,0:T(8,128)(2,1)} %fusion.6, bf16[1,1024,1024]{2,1,0:T(8,128)(2,1)S(1)} %copy-done, bf16[1,72,1024]{2,1,0:T(8,128)(2,1)S(1)} %copy-done.10), kind=kOutput, calls=%fused_computation.20 | convolution fusion | flops 9215180800 | bytes 11223040 | tf_op jit(solution)/shard_map/qigc,lg->qilc/dot_general | solution.py:49
  50.0 5.2 %all-to-all-start.1 = ((bf16[16,2,72,128]{3,2,1,0:T(8,128)(2,1)}), bf16[16,2,72,128]{3,2,1,0:T(8,128)(2,1)S(1)}, u32[]{:S(2)}, u32[]{:S(2)}) async-start(bf16[16,2,72,128]{3,2,1,0:T(8,128)(2,1)} %fusion.17), calls=%async_computation.1 | async-start | bytes 1179648 | tf_op jit(solution)/shard_map/all_to_all | solution.py:52
  55.1 1.2 fusion.49
  56.4 0.0 copy-done.7
  56.4 0.6 broadcast_multiply_fusion
  56.9 0.0 copy-done.8
  56.9 0.7 iota_compare_fusion.5
  57.6 9.5 %all-to-all-done.1 = bf16[16,2,72,128]{3,2,1,0:T(8,128)(2,1)S(1)} async-done(((bf16[16,2,72,128]{3,2,1,0:T(8,128)(2,1)}), bf16[16,2,72,128]{3,2,1,0:T(8,128)(2,1)S(1)}, u32[]{:S(2)}, u32[]{:S(2)}) %all-to-all-start.1) | async-done | bytes 589856 | tf_op jit(solution)/shard_map/all_to_all | solution.py:52
  67.1 4.5 %all-to-all-start.3 = ((bf16[16,16,1,256]{3,1,2,0:T(8,128)(2,1)}), bf16[16,16,1,256]{3,1,2,0:T(8,128)(2,1)S(1)}, u32[]{:S(2)}, u32[]{:S(2)}) async-start(bf16[16,16,1,256]{3,1,2,0:T(8,128)(2,1)} %copy.74), calls=%async_computation.3 | async-start | bytes 262144 | tf_op jit(solution)/shard_map/all_to_all | solution.py:97
  71.6 1.7 %convert_multiply_fusion = (f32[72,16,128]{2,1,0:T(8,128)S(1)}, bf16[72,16,128]{2,1,0:T(8,128)(2,1)}) fusion(s32[16]{0:T(128)} %copy-done.6, bf16[32,72,128]{2,1,0:T(8,128)(2,1)S(1)} %bitcast.167, pred[16,128]{1,0:T(8,128)(4,1)} %iota_compare_fusion.5), kind=kOutput, calls=%fused_computation.43 | convolution fusion | flops 10027520 | bytes 1476672 | tf_op jit(solution)/shard_map/bd,dlc->lbc/dot_general | solution.py:55
  73.3 0.1 reshape.106
  73.4 0.0 copy-start.1
  73.4 0.0 copy-start.5
  73.4 4.3 %fusion.30 = bf16[72,2,256]{2,0,1:T(8,128)(2,1)S(1)} fusion(f32[72,2048,1]{1,0,2:T(8,128)S(1)} %reshape.106, f32[2,256,2048]{2,1,0:T(8,128)} %constant.45.clone), kind=kOutput, calls=%fused_computation.39 | convolution fusion | flops 453058560 | bytes 4857856 | tf_op jit(solution)/shard_map/lx,rmx->rml/dot_general | solution.py:85
  77.7 0.9 fusion.34
  78.6 0.9 pad_maximum_fusion
  79.5 0.9 copy.48
  80.4 0.0 all-to-all-done.3
  80.4 14.5 %all-to-all-start.2 = ((bf16[256,4,72]{2,1,0:T(4,128)(2,1)}), bf16[256,4,72]{2,1,0:T(4,128)(2,1)S(1)}, u32[]{:S(2)}, u32[]{:S(2)}) async-start(bf16[256,4,72]{2,1,0:T(4,128)(2,1)} %copy.48), calls=%async_computation.2 | async-start | bytes 524288 | tf_op jit(solution)/shard_map/all_to_all | solution.py:94
  94.9 0.1 maximum_multiply_fusion
  95.0 0.8 add_divide_fusion
  95.8 14.6 %all-to-all-done.2 = bf16[256,4,72]{2,1,0:T(4,128)(2,1)S(1)} async-done(((bf16[256,4,72]{2,1,0:T(4,128)(2,1)}), bf16[256,4,72]{2,1,0:T(4,128)(2,1)S(1)}, u32[]{:S(2)}, u32[]{:S(2)}) %all-to-all-start.2) | async-done | bytes 147488 | tf_op jit(solution)/shard_map/all_to_all | solution.py:94
  110.4 0.2 copy.49
  110.6 0.0 copy-done.2
  110.6 0.9 fusion.23
  111.4 0.2 fusion.27
  111.7 0.9 fusion.25
  112.6 0.2 fusion.31
  112.8 0.8 copy.53
  113.6 5.9 %all-to-all-start.4 = ((bf16[256,2,72]{2,1,0:T(2,128)(2,1)}), bf16[256,2,72]{2,1,0:T(2,128)(2,1)S(1)}, u32[]{:S(2)}, u32[]{:S(2)}) async-start(bf16[256,2,72]{2,1,0:T(2,128)(2,1)} %copy.53), calls=%async_computation.4 | async-start | bytes 262144 | tf_op jit(solution)/shard_map/all_to_all | solution.py:121
  119.5 0.0 copy-done.1
  119.5 0.8 reshape.97
  120.4 11.9 %all-to-all-done.4 = bf16[256,2,72]{2,1,0:T(2,128)(2,1)S(1)} async-done(((bf16[256,2,72]{2,1,0:T(2,128)(2,1)}), bf16[256,2,72]{2,1,0:T(2,128)(2,1)S(1)}, u32[]{:S(2)}, u32[]{:S(2)}) %all-to-all-start.4) | async-done | bytes 73760 | tf_op jit(solution)/shard_map/all_to_all | solution.py:121
  132.3 0.0 copy-done.5
  132.3 0.3 convolution_bitcast_fusion.2
  132.6 3.6 %fusion.11 = f32[72,1,2048]{2,0,1:T(8,128)S(1)} fusion(f32[2,256,72]{1,2,0:T(8,128)S(1)} %convolution_bitcast_fusion.2, f32[2,256,2048]{2,1,0:T(8,128)} %constant.45.clone), kind=kOutput, calls=%fused_computation.16 | convolution fusion | flops 453132288 | bytes 4931584 | tf_op jit(solution)/shard_map/rml,rmx->lx/dot_general | solution.py:123
  136.2 1.4 %copy.55 = f32[72,1,2048]{2,1,0:T(1,128)} copy(f32[72,1,2048]{2,0,1:T(8,128)S(1)} %fusion.11) | data formatting | bytes 1179648
  (5 shorter events, 0.1 us)
Async XLA Ops:
  0.6 33.2 %copy-start = (bf16[1,1024,1024]{2,1,0:T(8,128)(2,1)S(1)}, bf16[1,1024,1024]{2,1,0:T(8,128)(2,1)}, u32[]{:S(2)}) copy-start(bf16[1,1024,1024]{2,1,0:T(8,128)(2,1)} %param.21) | copy-start | bytes 6291460
  0.6 22.5 %copy-start.4 = (s32[256]{0:T(256)S(1)}, s32[256]{0:T(256)}, u32[]{:S(2)}) copy-start(s32[256]{0:T(256)} %param.17) | copy-start | bytes 3076
  0.7 23.4 %copy-start.3 = (f32[16,16,1,256]{3,2,1,0:T(1,128)S(1)}, f32[16,16,1,256]{3,2,1,0:T(1,128)}, u32[]{:S(2)}) copy-start(f32[16,16,1,256]{3,2,1,0:T(1,128)} %param.15) | copy-start | bytes 786436
  0.7 26.3 %copy-start.9 = (bf16[1,72,1024]{2,1,0:T(8,128)(2,1)S(1)}, bf16[1,72,1024]{2,1,0:T(8,128)(2,1)}, u32[]{:S(2)}) copy-start(bf16[1,72,1024]{2,1,0:T(8,128)(2,1)} %param.20) | copy-start | bytes 442372
  2.3 3.1 %copy-start.6 = (s32[16]{0:T(128)}, s32[16]{0:T(128)S(1)}, u32[]{:S(2)}) copy-start(s32[16]{0:T(128)S(1)} %fusion.50) | copy-start | bytes 196
  6.5 20.4 %all-to-all-start = ((bf16[16,2,72,128]{3,2,1,0:T(8,128)(2,1)}), bf16[16,2,72,128]{3,2,1,0:T(8,128)(2,1)S(1)}, u32[]{:S(2)}, u32[]{:S(2)}) async-start(bf16[16,2,72,128]{3,2,1,0:T(8,128)(2,1)} %copy.45), calls=%async_computation | async-start | bytes 1179648 | tf_op jit(solution)/shard_map/all_to_all | solution.py:42
  24.7 9.1 %copy-start.10 = (bf16[1,72,1024]{2,1,0:T(8,128)(2,1)S(1)}, bf16[1,72,1024]{2,1,0:T(8,128)(2,1)}, u32[]{:S(2)}) copy-start(bf16[1,72,1024]{2,1,0:T(8,128)(2,1)} %param.22) | copy-start | bytes 442372
  33.9 22.5 %copy-start.7 = (f32[72]{0:T(128)S(1)}, f32[72]{0:T(128)}, u32[]{:S(2)}) copy-start(f32[72]{0:T(128)} %param.16) | copy-start | bytes 868
  33.9 23.1 %copy-start.8 = (s32[16]{0:T(128)S(1)}, s32[16]{0:T(128)}, u32[]{:S(2)}) copy-start(s32[16]{0:T(128)} %param.18) | copy-start | bytes 196
  50.0 60.6 %copy-start.2 = (f32[72,2,1,256]{3,2,1,0:T(1,128)S(1)}, f32[72,2,1,256]{3,2,1,0:T(1,128)}, u32[]{:S(2)}) copy-start(f32[72,2,1,256]{3,2,1,0:T(1,128)} %param.14) | copy-start | bytes 442372
  50.0 17.2 %all-to-all-start.1 = ((bf16[16,2,72,128]{3,2,1,0:T(8,128)(2,1)}), bf16[16,2,72,128]{3,2,1,0:T(8,128)(2,1)S(1)}, u32[]{:S(2)}, u32[]{:S(2)}) async-start(bf16[16,2,72,128]{3,2,1,0:T(8,128)(2,1)} %fusion.17), calls=%async_computation.1 | async-start | bytes 1179648 | tf_op jit(solution)/shard_map/all_to_all | solution.py:52
  67.1 13.3 %all-to-all-start.3 = ((bf16[16,16,1,256]{3,1,2,0:T(8,128)(2,1)}), bf16[16,16,1,256]{3,1,2,0:T(8,128)(2,1)S(1)}, u32[]{:S(2)}, u32[]{:S(2)}) async-start(bf16[16,16,1,256]{3,1,2,0:T(8,128)(2,1)} %copy.74), calls=%async_computation.3 | async-start | bytes 262144 | tf_op jit(solution)/shard_map/all_to_all | solution.py:97
  73.4 46.2 %copy-start.1 = (bf16[72,16,128]{2,1,0:T(8,128)(2,1)S(1)}, bf16[72,16,128]{2,1,0:T(8,128)(2,1)}, u32[]{:S(2)}) copy-start(bf16[72,16,128]{2,1,0:T(8,128)(2,1)} %get-tuple-element.13) | copy-start | bytes 884740
  73.4 58.9 %copy-start.5 = (s32[256]{0:T(256)S(1)}, s32[256]{0:T(256)}, u32[]{:S(2)}) copy-start(s32[256]{0:T(256)} %param.17) | copy-start | bytes 3076
  80.4 30.0 %all-to-all-start.2 = ((bf16[256,4,72]{2,1,0:T(4,128)(2,1)}), bf16[256,4,72]{2,1,0:T(4,128)(2,1)S(1)}, u32[]{:S(2)}, u32[]{:S(2)}) async-start(bf16[256,4,72]{2,1,0:T(4,128)(2,1)} %copy.48), calls=%async_computation.2 | async-start | bytes 524288 | tf_op jit(solution)/shard_map/all_to_all | solution.py:94
  113.6 18.7 %all-to-all-start.4 = ((bf16[256,2,72]{2,1,0:T(2,128)(2,1)}), bf16[256,2,72]{2,1,0:T(2,128)(2,1)S(1)}, u32[]{:S(2)}, u32[]{:S(2)}) async-start(bf16[256,2,72]{2,1,0:T(2,128)(2,1)} %copy.53), calls=%async_computation.4 | async-start | bytes 262144 | tf_op jit(solution)/shard_map/all_to_all | solution.py:121
where the time goes:
time: 138 us
  matrix products  40.9 us (30%)
  starting transfers between devices  38.5 us (28%)
  waiting for transfers between devices  38.2 us (28%)
  other arithmetic  11.2 us (8%)
  local copies, waits for them, and re-layouts  7.28 us (5%)
  between operations  1.5 us (1%)
    dot_general x1, matrix products, physics_local(): jnp.einsum('qigc,lg->qilc', hidden_two, w_out[0], preferred_element_type=...  16.1 us
    all_to_all x1, waiting for transfers between devices, on_device(): got = lax.all_to_all(sent, BOTH, split_axis=0, concat_axis=0, tiled=True)  14.6 us
    all_to_all x1, starting transfers between devices, on_device(): got = lax.all_to_all(sent, BOTH, split_axis=0, concat_axis=0, tiled=True)  14.5 us
    all_to_all x1, waiting for transfers between devices, on_device(): lax.all_to_all(back.astype(jnp.bfloat16), BOTH, split_axis=0, concat_axis...  11.9 us
    all_to_all x1, waiting for transfers between devices, physics_local(): lax.all_to_all(computed, 'phys', split_axis=0, concat_axis=0, tiled=True)  9.52 us
    dot_general x2, matrix products, to_slots(): jnp.einsum('lx,rmx->rml', field, table, precision=HIGH)  8.53 us
    all_to_all x1, starting transfers between devices, physics_local(): lax.all_to_all(outgoing, 'phys', split_axis=0, concat_axis=0, tiled=True)  8.44 us
    dot_general x1, matrix products, physics_local(): jnp.einsum('qilc,lh->qihc', arrived, w_in[0], preferred_element_type=jnp....  6.91 us
  transfers between devices with their start and end apart: 5, of which 4 were waited for; matrix products, arithmetic and copies ran while one was open for 16% of the time, Pallas kernels for 0%

commit v1 on v0

v1 whole, which is shorter than its diff:
```python
import functools
import math

import jax
import jax.numpy as jnp
import numpy as np
from jax import lax
from jax.experimental import pallas as pl
from jax.experimental.pallas import tpu as pltpu
from jax.sharding import PartitionSpec as P

NB_ROW = 16
CMAX = 128
CAP = 2
LANES = 128
TIME_STEP = 0.5
BOTH = ("dyn", "phys")
VMEM = pl.BlockSpec(memory_space=pltpu.VMEM)
SMEM = pl.BlockSpec(memory_space=pltpu.SMEM)
BF16 = jnp.bfloat16
F32 = jnp.float32


def params():
    return pltpu.CompilerParams(vmem_limit_bytes=48 << 20)


def wave_table(waves, n_lon):
    phases = np.arange(waves)[:, None] * np.arange(n_lon)[None, :] % n_lon
    angles = phases.astype(np.float64) * (2.0 * math.pi / n_lon)
    table = np.concatenate([np.cos(angles), -np.sin(angles)], axis=0).astype(np.float32)
    high = table.astype(jnp.bfloat16)
    low = (table - high.astype(np.float32)).astype(jnp.bfloat16)
    return high, low


def dot(a, b):
    return jnp.dot(a, b, preferred_element_type=F32)


def dot_nt(a, b):
    return lax.dot_general(a, b, (((1,), (1,)), ((), ())), preferred_element_type=F32)


def dot_tn(a, b):
    return lax.dot_general(a, b, (((0,), (0,)), ((), ())), preferred_element_type=F32)


def split(value):
    high = value.astype(BF16)
    return high, (value - high.astype(F32)).astype(BF16)


def place_kernel(expert_ref, state_ref, legendre_ref, out_ref, count_ref):
    networks, _, width = out_ref.shape
    blocks = state_ref.shape[1]
    share = legendre_ref.shape[1] // CAP
    out_ref[:, share:, :] = jnp.zeros((networks, out_ref.shape[1] - share, width), BF16)
    for network in range(networks):
        count_ref[network] = 0
        for half in range(CAP):
            part = legendre_ref[network, pl.ds(half, share, stride=CAP), :]
            out_ref[network, :share, half * CMAX : (half + 1) * CMAX] = part.astype(BF16)
    for block in range(blocks):
        network = expert_ref[block]
        rank = count_ref[network]
        count_ref[network] = rank + 1
        lanes = pl.ds(pl.multiple_of(rank * CMAX, CMAX), CMAX)
        out_ref[network, share:, lanes] = state_ref[:, block, :].astype(BF16)


def place_blocks(experts, state, legendre):
    levels = state.shape[0]
    networks, share, _ = legendre.shape
    return pl.pallas_call(
        place_kernel,
        in_specs=[SMEM, VMEM, VMEM],
        out_specs=VMEM,
        out_shape=jax.ShapeDtypeStruct((networks, share // CAP + levels, CAP * CMAX), BF16),
        scratch_shapes=[pltpu.SMEM((networks,), jnp.int32)],
        compiler_params=params(),
        name="place",
    )(experts, state, legendre)


def first_kernel(n_lon, state_ref, prev_ref, order_ref, high_ref, low_ref, table_ref, out_ref):
    levels, blocks, _ = state_ref.shape
    waves = order_ref.shape[0]
    parts = [
        state_ref[:, block, :] + TIME_STEP * prev_ref[:, block, :] for block in range(blocks)
    ]
    forcing = jnp.concatenate(parts, axis=1)
    blank = jnp.zeros((LANES - levels, n_lon), F32)
    high, low = split(jnp.concatenate([forcing, blank], axis=0))
    both = dot_nt(high_ref[...], jnp.concatenate([high, low], axis=0))
    natural = both[:, :LANES] + (both[:, LANES:] + dot_nt(low_ref[...], high))
    natural = (natural * (1.0 / math.sqrt(n_lon))).astype(BF16)
    for part in range(2):
        rows = slice(part * waves, (part + 1) * waves)
        table_ref[rows, :] = dot(order_ref[...], high_ref[rows, :]).astype(BF16)
        out_ref[rows, :] = dot(order_ref[...], natural[rows, :]).astype(BF16)


def first_transform(state, prev, order, high, low):
    rows, n_lon = high.shape
    return pl.pallas_call(
        functools.partial(first_kernel, n_lon),
        in_specs=[VMEM] * 5,
        out_specs=[VMEM] * 2,
        out_shape=[
            jax.ShapeDtypeStruct((rows, n_lon), BF16),
            jax.ShapeDtypeStruct((rows, LANES), BF16),
        ],
        compiler_params=params(),
        cost_estimate=pl.CostEstimate(
            flops=4 * rows * n_lon * rows, bytes_accessed=8 << 20, transcendentals=0
        ),
        name="first",
    )(state, prev, order, high, low)


def half_silu(half):
    return (half + half * jnp.tanh(half)).astype(BF16)


def network_kernel(skip, group, x_ref, first_ref, middle_ref, last_ref, out_ref):
    width = x_ref.shape[2]
    for start in range(0, x_ref.shape[0], group):
        columns = jnp.concatenate([x_ref[start + i, skip:, :] for i in range(group)], axis=1)
        one = half_silu(dot(first_ref[...], columns))
        two = half_silu(dot(middle_ref[...], one))
        out = dot(last_ref[...], two).astype(BF16)
        for i in range(group):
            out_ref[start + i] = out[:, i * width : (i + 1) * width]


def network(arrived, first_w, middle_w, last_w):
    senders, rows, width = arrived.shape
    levels, hidden = last_w.shape
    step = 4
    return pl.pallas_call(
        functools.partial(network_kernel, rows - levels, 2),
        grid=(senders // step,),
        in_specs=[
            pl.BlockSpec((step, rows, width), lambda i: (i, 0, 0)),
            pl.BlockSpec((hidden, levels), lambda i: (0, 0)),
            pl.BlockSpec((hidden, hidden), lambda i: (0, 0)),
            pl.BlockSpec((levels, hidden), lambda i: (0, 0)),
        ],
        out_specs=pl.BlockSpec((step, levels, width), lambda i: (i, 0, 0)),
        out_shape=jax.ShapeDtypeStruct((senders, levels, width), BF16),
        compiler_params=params(),
        cost_estimate=pl.CostEstimate(
            flops=2 * senders * width * hidden * (hidden + 2 * 256),
            bytes_accessed=4 << 20,
            transcendentals=2 * senders * width * hidden,
        ),
        name="network",
    )(arrived, first_w, middle_w, last_w)


def return_kernel(
    n_lon, expert_ref, cloudy_ref, returned_ref, table_ref, first_ref, tend_ref, out_ref, count_ref, rows_ref
):
    networks, levels, _ = returned_ref.shape
    waves = first_ref.shape[0] // 2
    lanes = lax.broadcasted_iota(jnp.int32, (levels, CMAX), 1)
    for network in range(networks):
        count_ref[network] = 0
    for block in range(NB_ROW):
        network = expert_ref[block]
        rank = count_ref[network]
        count_ref[network] = rank + 1
        place = pl.ds(pl.multiple_of(rank * CMAX, CMAX), CMAX)
        values = returned_ref[network, :, place].astype(F32)
        kept = jnp.where(lanes < cloudy_ref[block], values, 0.0)
        tend_ref[:, block * CMAX : (block + 1) * CMAX] = kept.astype(BF16)
    out = dot_nt(table_ref[...], tend_ref[...]) * (TIME_STEP / math.sqrt(n_lon))
    out = jnp.concatenate([out, jnp.zeros((out.shape[0], LANES - levels), F32)], axis=1)
    for part in range(2):
        rows = slice(part * waves, (part + 1) * waves)
        rows_ref[pl.ds(part, waves, stride=4), :] = first_ref[rows, :].astype(F32)
        rows_ref[pl.ds(2 + part, waves, stride=4), :] = out[rows]
    out_ref[...] = rows_ref[...].astype(BF16)


def return_blocks(experts, cloudy, returned, table, first):
    rows, n_lon = table.shape
    networks, levels, _ = returned.shape
    return pl.pallas_call(
        functools.partial(return_kernel, n_lon),
        in_specs=[SMEM, SMEM, VMEM, VMEM, VMEM],
        out_specs=[VMEM] * 2,
        out_shape=[
            jax.ShapeDtypeStruct((levels, n_lon), BF16),
            jax.ShapeDtypeStruct((2 * rows, LANES), BF16),
        ],
        scratch_shapes=[pltpu.SMEM((networks,), jnp.int32), pltpu.VMEM((2 * rows, LANES), F32)],
        compiler_params=params(),
        name="return",
    )(experts, cloudy, returned, table, first)


def solve_kernel(got_ref, there_ref, back_ref, gain_ref, pull_ref, regain_ref, out_ref, rows_ref, turn_ref):
    lats = back_ref.shape[0]
    rows_ref[...] = got_ref[...].astype(F32)
    parts = [rows_ref[pl.ds(part, lats, stride=4), :].astype(BF16) for part in range(4)]

    def twice(table_ref, value):
        both = dot(table_ref[...], jnp.concatenate(split(value), axis=1))
        return both[:, : 2 * LANES] + both[:, 2 * LANES :]

    spectral = dot(there_ref[...], jnp.concatenate(parts, axis=1))
    gain = gain_ref[...]
    pull = pull_ref[...]
    back = twice(back_ref, spectral[:, : 2 * LANES] * gain + pull)
    again = spectral[:, 2 * LANES :] + twice(there_ref, back * regain_ref[...])
    final = twice(back_ref, again * gain + pull)
    for part in range(2):
        turn_ref[pl.ds(part, lats, stride=2), :] = final[:, part * LANES : (part + 1) * LANES]
    out_ref[...] = turn_ref[...].astype(BF16)


def solve_twice(got, there, back, gain, pull, regain):
    rows = got.shape[0]
    return pl.pallas_call(
        solve_kernel,
        in_specs=[VMEM] * 6,
        out_specs=VMEM,
        out_shape=jax.ShapeDtypeStruct((rows // 2, LANES), BF16),
        scratch_shapes=[pltpu.VMEM((rows, LANES), F32), pltpu.VMEM((rows // 2, LANES), F32)],
        compiler_params=params(),
        name="solve",
    )(got, there, back, gain, pull, regain)


def synthesis_kernel(scale, home_ref, table_ref, out_ref, rows_ref):
    levels, blocks, width = out_ref.shape
    waves = home_ref.shape[0] // 2
    rows_ref[...] = home_ref[...].astype(F32)
    parts = [rows_ref[pl.ds(part, waves, stride=2), :].astype(BF16) for part in range(2)]
    grid = dot_tn(jnp.concatenate(parts, axis=0), table_ref[...]) * scale
    for block in range(blocks):
        out_ref[:, block, :] = grid[:levels, block * width : (block + 1) * width]


def synthesis(home, table, levels, scale):
    n_lon = table.shape[1]
    return pl.pallas_call(
        functools.partial(synthesis_kernel, scale),
        in_specs=[VMEM] * 2,
        out_specs=VMEM,
        out_shape=jax.ShapeDtypeStruct((levels, NB_ROW, n_lon // NB_ROW), F32),
        scratch_shapes=[pltpu.VMEM(home.shape, F32)],
        compiler_params=params(),
        name="synthesis",
    )(home, table)


def on_device(
    initial_state,
    prev_tendency,
    analysis,
    legendre,
    nudge_rate,
    band_waves,
    cloudy_count,
    expert_of,
    w_in,
    w_mid,
    w_out,
):
    levels, _, n_lon = initial_state.shape
    n_phys = lax.axis_size("phys")
    waves = band_waves.shape[0]
    coeffs = legendre.shape[3]
    lats = waves
    rows = 2 * waves
    state = initial_state.reshape(levels, NB_ROW, n_lon // NB_ROW)
    prev = prev_tendency.reshape(levels, NB_ROW, n_lon // NB_ROW)
    experts = expert_of[:, 0]

    share = lats // n_phys

    outgoing = place_blocks(experts, state, legendre.reshape(n_phys, share * CAP, coeffs // CAP))
    arrived = lax.all_to_all(outgoing, "phys", split_axis=0, concat_axis=0, tiled=True)
    first_w = (w_in[0] * 0.5).T
    middle_w = (w_mid[0] * 0.5).T
    computed = network(arrived, first_w, middle_w, w_out[0])
    returned = lax.all_to_all(computed, "phys", split_axis=0, concat_axis=0, tiled=True)

    state, prev, analysis, band_waves, computed = lax.optimization_barrier(
        (state, prev, analysis, band_waves, computed)
    )
    high, low = (jnp.asarray(part) for part in wave_table(waves, n_lon))
    order = (band_waves[:, None] == jnp.arange(waves, dtype=jnp.int32)[None, :]).astype(BF16)
    table, first = first_transform(state, prev, order, high, low)
    back_table = arrived[:, :share, :].transpose(1, 0, 2).reshape(lats, coeffs)
    there_table = back_table.T
    me = lax.axis_index("dyn") * n_phys + lax.axis_index("phys")
    own_wave = lax.dynamic_index_in_dim(band_waves, me, 0, keepdims=False)
    total_wave = (own_wave + jnp.arange(coeffs, dtype=jnp.int32)).astype(F32)
    damping = total_wave * (total_wave + 1.0) / (waves * (waves + 1.0))
    rate = jnp.pad(nudge_rate, (0, LANES - levels))
    rate = jnp.concatenate([rate, rate])[None, :]
    inverse = 1.0 / (1.0 + TIME_STEP * (damping[:, None] + rate))
    pulled = jnp.pad(analysis[:, :, 0].transpose(2, 1, 0), ((0, 0), (0, 0), (0, LANES - levels)))
    pulled = pulled.reshape(coeffs, 2 * LANES) * (TIME_STEP * rate) * inverse
    gain = inverse * (1.0 / math.sqrt(lats) / math.sqrt(coeffs))
    pull = pulled * (1.0 / math.sqrt(coeffs))
    again = (n_lon / 2.0) / math.sqrt(waves) / math.sqrt(n_lon)
    zero_wave = own_wave == 0
    regain = jnp.stack([jnp.where(zero_wave, 2.0 * again, again), jnp.where(zero_wave, 0.0, again)])
    regain = jnp.repeat(regain, LANES)[None, :]

    tendency, sent = return_blocks(experts, cloudy_count, returned, table, first)
    got = lax.all_to_all(
        sent.reshape(waves, 4, LANES), BOTH, split_axis=0, concat_axis=0, tiled=True
    )
    back = solve_twice(got.reshape(4 * lats, LANES), there_table, back_table, gain, pull, regain)
    home = lax.all_to_all(
        back.reshape(lats, 2, LANES), BOTH, split_axis=0, concat_axis=0, tiled=True
    )
    final = synthesis(home.reshape(rows, LANES), table, levels, 1.0 / math.sqrt(waves))
    return (final.reshape(levels, 1, n_lon), tendency.reshape(levels, 1, n_lon))


def solution(mesh):
    in_specs = (
        P(None, ("dyn", "phys"), None),
        P(None, ("dyn", "phys"), None),
        P(None, None, ("dyn", "phys"), None),
        P("dyn", None, "phys", None),
        P(),
        P(),
        P(("dyn", "phys")),
        P(("dyn", "phys"), None),
        P("phys", None, None),
        P("phys", None, None),
        P("phys", None, None),
    )
    out_specs = (P(None, ("dyn", "phys"), None), P(None, ("dyn", "phys"), None))
    return jax.shard_map(
        on_device, mesh=mesh, in_specs=in_specs, out_specs=out_specs, check_vma=False
    )
```

time: 138 us -> 109 us (0.79)
  matrix products: 40.9 us -> 0 us
  Pallas kernels: 0 us -> 23.1 us
  blocking collectives: 0 us -> 18.5 us
  starting transfers between devices: 38.5 us -> 23.7 us
  waiting for transfers between devices: 38.2 us -> 24 us
  other arithmetic: 11.2 us -> 3.72 us
  local copies, waits for them, and re-layouts: 7.28 us -> 13.4 us
    dot_general x12 -> x0, matrix products: 39.7 us -> none  [the longest x1 16.1 us: physics_local(): jnp.einsum('qigc,lg->qilc', hidden_two, w_out[0], preferred_element_type=...]
    pallas_call x0 -> x6, Pallas kernels: none -> 23.1 us  [the longest x1 12.9 us: network(): pl.pallas_call(functools.partial(network_kernel, rows - levels, 2), grid=...]
    all_to_all x0 -> x1, blocking collectives: none -> 18.5 us  [on_device(): lax.all_to_all(back.reshape(lats, 2, LANES), BOTH, split_axis=0, concat_a...]
    all_to_all x5 -> x3, starting transfers between devices: 38.5 us -> 23.7 us  [the longest x1 11 us: on_device(): lax.all_to_all(sent.reshape(waves, 4, LANES), BOTH, split_axis=0, concat_...]
    all_to_all x5 -> x3, waiting for transfers between devices: 38.2 us -> 24 us  [the longest x1 10.4 us: on_device(): lax.all_to_all(sent.reshape(waves, 4, LANES), BOTH, split_axis=0, concat_...]
    unnamed x25 -> x32, local copies, waits for them, and re-layouts: 2.18 us -> 10.7 us
    convert_element_type x3 -> x1, other arithmetic: 3.27 us -> 0.1 us  [on_device(): (band_waves[:, None] == jnp.arange(waves, dtype=jnp.int32)[None, :]).asty...]
    add x1 -> x0, other arithmetic: 2.01 us -> none  [on_device(): first = to_slots(initial_state[:, 0] + TIME_STEP * prev_tendency[:, 0])]
  transfers between devices with their start and end apart: 5 -> 3, of which waited for: 4 -> 3; matrix products, arithmetic and copies ran while one was open for 16% -> 8% of each run, Pallas kernels for 0% -> 3%
where the time goes in v1:
time: 109 us; the launch traced here: 108 us
  waiting for transfers between devices  24 us (22%)
  starting transfers between devices  23.7 us (22%)
  Pallas kernels  23.1 us (21%)
  blocking collectives  18.5 us (17%)
  local copies, waits for them, and re-layouts  13.4 us (12%)
  other arithmetic  3.72 us (3%)
  between operations  1.44 us (1%)
    all_to_all x1, blocking collectives, on_device(): lax.all_to_all(back.reshape(lats, 2, LANES), BOTH, split_axis=0, concat_a...  18.5 us
    pallas_call x1, Pallas kernels, network(): pl.pallas_call(functools.partial(network_kernel, rows - levels, 2), grid=...  12.9 us
    all_to_all x1, starting transfers between devices, on_device(): lax.all_to_all(sent.reshape(waves, 4, LANES), BOTH, split_axis=0, concat_...  11 us
    unnamed x32, local copies, waits for them, and re-layouts  10.7 us
    all_to_all x1, waiting for transfers between devices, on_device(): lax.all_to_all(sent.reshape(waves, 4, LANES), BOTH, split_axis=0, concat_...  10.4 us
    all_to_all x1, waiting for transfers between devices, on_device(): lax.all_to_all(outgoing, 'phys', split_axis=0, concat_axis=0, tiled=True)  9.08 us
    all_to_all x1, starting transfers between devices, on_device(): lax.all_to_all(outgoing, 'phys', split_axis=0, concat_axis=0, tiled=True)  8.45 us
    all_to_all x1, waiting for transfers between devices, on_device(): lax.all_to_all(computed, 'phys', split_axis=0, concat_axis=0, tiled=True)  4.59 us
  transfers between devices with their start and end apart: 3, of which 3 were waited for; matrix products, arithmetic and copies ran while one was open for 8% of the time, Pallas kernels for 3%

profile of v1, /device:TPU:1, one launch (start us, length us, event | category | flops | bytes accessed | tf_op | source)
XLA Modules:
  0.0 107.9 jit_solution(1530081851074034214)
XLA Ops:
  0.6 0.0 copy-start
  0.6 1.1 copy-done
  1.7 0.0 copy-start.4
  1.7 0.9 copy-done.4
  2.6 0.0 copy-start.5
  2.7 0.7 copy-done.5
  3.3 0.0 copy-start.12
  3.3 0.0 copy-start.11
  3.3 2.0 %place.1 = bf16[16,88,256]{2,1,0:T(8,128)(2,1)} custom-call(s32[16]{0:T(128)S(1)} %bitcast.48, f32[72,16,128]{2,1,0:T(8,128)S(1)} %bitcast.42, f32[16,32,128]{2,1,0:T(8,128)S(1)} %bitcast.47), custom_call_target="tpu_custom_call" | custom-call | tf_op jit(solution)/shard_map/place/pallas_call | solution.py:75
  5.4 8.4 %all-to-all-start = ((bf16[16,88,256]{2,1,0:T(8,128)(2,1)}), bf16[16,88,256]{2,1,0:T(8,128)(2,1)S(1)}, u32[]{:S(2)}, u32[]{:S(2)}) async-start(bf16[16,88,256]{2,1,0:T(8,128)(2,1)} %place.1), calls=%async_computation | async-start | bytes 1441792 | tf_op jit(solution)/shard_map/all_to_all | solution.py:286
  13.8 0.0 copy-done.12
  13.8 0.2 copy.15
  14.0 0.0 copy-done.11
  14.0 2.6 %copy.16 = bf16[1,1024,1024]{1,2,0:T(8,128)(2,1)} copy(bf16[1,1024,1024]{2,1,0:T(8,128)(2,1)S(1)} %copy-done.11) | data formatting | bytes 4194304 | tf_op args[9]
  16.6 0.0 copy-start.9
  16.6 1.8 %multiply_bitcast_fusion.middle_ref = bf16[1024,1024]{1,0:T(8,128)(2,1)S(1)} fusion(bf16[1,1024,1024]{1,2,0:T(8,128)(2,1)} %copy.16), kind=kLoop, calls=%fused_computation | loop fusion | flops 1048576 | bytes 4194304 | tf_op jit(solution)/shard_map/transpose | solution.py:288
  18.4 9.1 %all-to-all-done.x_ref = bf16[16,88,256]{2,1,0:T(8,128)(2,1)S(1)} async-done(((bf16[16,88,256]{2,1,0:T(8,128)(2,1)}), bf16[16,88,256]{2,1,0:T(8,128)(2,1)S(1)}, u32[]{:S(2)}, u32[]{:S(2)}) %all-to-all-start) | async-done | bytes 720928 | tf_op jit(solution)/shard_map/all_to_all | solution.py:286
  27.5 0.0 copy-done.9
  27.5 0.0 copy-start.14
  27.5 0.0 copy-start.13
  27.5 12.9 %network.1 = bf16[16,72,256]{2,1,0:T(8,128)(2,1)S(1)} custom-call(bf16[16,88,256]{2,1,0:T(8,128)(2,1)S(1)} %all-to-all-done.x_ref, bf16[1024,72]{1,0:T(8,128)(2,1)S(1)} %multiply_bitcast_fusion.1.first_ref, bf16[1024,1024]{1,0:T(8,128)(2,1)S(1)} %multiply_bitcast_fusion.middle_ref, bf16[72,1024]{1,0:T(8,128)(2,1)S(1)} %bitcast.52), custom_call_target="tpu_custom_call" | custom-call | flops 12884901888 | bytes 4194304 | tf_op jit(solution)/shard_map/network/pallas_call | solution.py:141
  40.5 0.0 copy-start.2
  40.5 0.8 copy-done.2
  41.3 4.2 %all-to-all-start.1 = ((bf16[16,72,256]{2,1,0:T(8,128)(2,1)}), bf16[16,72,256]{2,1,0:T(8,128)(2,1)S(1)}, u32[]{:S(2)}, u32[]{:S(2)}) async-start(bf16[16,72,256]{2,1,0:T(8,128)(2,1)} %copy-done.2), calls=%async_computation.1 | async-start | bytes 1179648 | tf_op jit(solution)/shard_map/all_to_all | solution.py:290
  45.5 0.0 copy-done.14
  45.5 0.0 copy-done.13
  45.5 0.1 fusion.2.order_ref
  45.6 0.0 copy-start.1
  45.7 1.1 copy-done.1
  46.7 0.0 copy-start.8
  46.7 1.1 copy-done.8
  47.8 0.0 copy-start.10
  47.8 1.6 %copy-done.10 = bf16[512,2048]{1,0:T(8,128)(2,1)S(1)} copy-done((bf16[512,2048]{1,0:T(8,128)(2,1)S(1)}, bf16[512,2048]{1,0:T(8,128)(2,1)}, u32[]{:S(2)}) %copy-start.10) | copy-done | bytes 2097176
  49.4 0.0 copy-start.6
  49.4 0.0 copy-start.7
  49.4 3.6 %first.1 = (bf16[512,2048]{1,0:T(8,128)(2,1)S(1)}, bf16[512,128]{1,0:T(8,128)(2,1)S(1)}) custom-call(f32[72,16,128]{2,1,0:T(8,128)S(1)} %bitcast.43, f32[72,16,128]{2,1,0:T(8,128)S(1)} %bitcast.51, bf16[256,256]{1,0:T(8,128)(2,1)S(1)} %fusion.2.order_ref, bf16[512,2048]{1,0:T(8,128)(2,1)S(1)} %copy-done.10, bf16[512,2048]{1,0:T(8,128)(2,1)} %constant.44.clone.low_ref), custom_call_target="tpu_custom_call" | custom-call | flops 2147483648 | bytes 8388608 | tf_op jit(solution)/shard_map/first/pallas_call | solution.py:106
  53.0 4.6 %all-to-all-done.1.returned_ref = bf16[16,72,256]{2,1,0:T(8,128)(2,1)S(1)} async-done(((bf16[16,72,256]{2,1,0:T(8,128)(2,1)}), bf16[16,72,256]{2,1,0:T(8,128)(2,1)S(1)}, u32[]{:S(2)}, u32[]{:S(2)}) %all-to-all-start.1) | async-done | bytes 589856 | tf_op jit(solution)/shard_map/all_to_all | solution.py:290
  57.6 0.0 copy-done.6
  57.6 0.0 copy-done.7
  57.6 2.0 %return.1 = (bf16[72,2048]{1,0:T(8,128)(2,1)}, bf16[1024,128]{1,0:T(8,128)(2,1)S(1)}) custom-call(s32[16]{0:T(128)S(1)} %bitcast.49, s32[16]{0:T(128)S(1)} %copy-done.7, bf16[16,72,256]{2,1,0:T(8,128)(2,1)S(1)} %all-to-all-done.1.returned_ref, bf16[512,2048]{1,0:T(8,128)(2,1)S(1)} %get-tuple-element.13.table_ref, ...), custom_call_target="tpu_custom_call" | custom-call | tf_op jit(solution)/shard_map/return/pallas_call | solution.py:190
  59.6 0.0 copy-start.3
  59.6 0.7 copy-done.3
  60.3 11.0 %all-to-all-start.2 = ((bf16[256,4,128]{2,1,0:T(4,128)(2,1)}), bf16[256,4,128]{2,1,0:T(4,128)(2,1)S(1)}, u32[]{:S(2)}, u32[]{:S(2)}) async-start(bf16[256,4,128]{2,1,0:T(4,128)(2,1)} %bitcast.46), calls=%async_computation.2 | async-start | bytes 524288 | tf_op jit(solution)/shard_map/all_to_all | solution.py:317
  71.4 0.1 copy.19.there_ref
  71.5 1.1 copy.23
  72.5 0.8 pad.9.clone
  73.3 0.6 dynamic_slice.4
  74.6 0.1 pad_maximum_fusion.1
  74.7 0.6 broadcast_multiply_fusion
  75.3 1.1 %fusion.1 = (f32[256,256]{1,0:T(8,128)S(1)}, f32[256,256]{1,0:T(8,128)S(1)}) fusion(f32[32,8,2,128]{3,2,1,0:T(2,128)} %bitcast.53, f32[256]{0:T(256)S(1)} %get-tuple-element.22, f32[256]{0:T(256)S(1)} %get-tuple-element.23, f32[256]{0:T(256)S(1)} %get-tuple-element.24), kind=kLoop, calls=%fused_computation.3 | loop fusion | flops 524288 | bytes 789504 | tf_op jit(solution)/shard_map/mul | solution.py:310
  76.4 10.4 %all-to-all-done.2 = bf16[256,4,128]{2,1,0:T(4,128)(2,1)S(1)} async-done(((bf16[256,4,128]{2,1,0:T(4,128)(2,1)}), bf16[256,4,128]{2,1,0:T(4,128)(2,1)S(1)}, u32[]{:S(2)}, u32[]{:S(2)}) %all-to-all-start.2) | async-done | bytes 262176 | tf_op jit(solution)/shard_map/all_to_all | solution.py:317
  86.8 0.1 broadcast_in_dim.2
  86.9 1.0 solve.1
  87.9 18.5 %all_to_all.20 = bf16[256,2,128]{2,1,0:T(2,128)(2,1)S(1)} all-to-all(bf16[256,2,128]{2,1,0:T(2,128)(2,1)S(1)} %bitcast.45), channel_id=1, replica_groups=mesh['dyn'=16,'phys'=16] {'dyn','phys'}, dimensions={0} | all-to-all | bytes 262144 | tf_op jit(solution)/shard_map/all_to_all | solution.py:321
  106.4 1.5 %synthesis.1 = f32[72,16,128]{2,1,0:T(8,128)} custom-call(bf16[512,128]{1,0:T(8,128)(2,1)S(1)} %bitcast.44, bf16[512,2048]{1,0:T(8,128)(2,1)S(1)} %get-tuple-element.13.table_ref), custom_call_target="tpu_custom_call" | custom-call | tf_op jit(solution)/shard_map/synthesis/pallas_call | solution.py:249
  (4 shorter events, 0.1 us)
Async XLA Ops:
  0.6 1.1 copy-start
  1.7 0.9 copy-start.4
  2.6 0.7 copy-start.5
  3.3 10.5 %copy-start.12 = (bf16[1,72,1024]{2,1,0:T(8,128)(2,1)S(1)}, bf16[1,72,1024]{2,1,0:T(8,128)(2,1)}, u32[]{:S(2)}) copy-start(bf16[1,72,1024]{2,1,0:T(8,128)(2,1)} %param.21) | copy-start | bytes 442372
  3.3 10.7 %copy-start.11 = (bf16[1,1024,1024]{2,1,0:T(8,128)(2,1)S(1)}, bf16[1,1024,1024]{2,1,0:T(8,128)(2,1)}, u32[]{:S(2)}) copy-start(bf16[1,1024,1024]{2,1,0:T(8,128)(2,1)} %param.22) | copy-start | bytes 6291460
  5.4 22.1 %all-to-all-start = ((bf16[16,88,256]{2,1,0:T(8,128)(2,1)}), bf16[16,88,256]{2,1,0:T(8,128)(2,1)S(1)}, u32[]{:S(2)}, u32[]{:S(2)}) async-start(bf16[16,88,256]{2,1,0:T(8,128)(2,1)} %place.1), calls=%async_computation | async-start | bytes 1441792 | tf_op jit(solution)/shard_map/all_to_all | solution.py:286
  16.6 10.9 %copy-start.9 = (bf16[1,72,1024]{2,1,0:T(8,128)(2,1)S(1)}, bf16[1,72,1024]{2,1,0:T(8,128)(2,1)}, u32[]{:S(2)}) copy-start(bf16[1,72,1024]{2,1,0:T(8,128)(2,1)} %param.23) | copy-start | bytes 442372
  27.5 18.0 %copy-start.14 = (f32[72]{0:T(128)S(1)}, f32[72]{0:T(128)}, u32[]{:S(2)}) copy-start(f32[72]{0:T(128)} %param.17) | copy-start | bytes 868
  27.5 18.0 %copy-start.13 = (s32[256]{0:T(256)S(1)}, s32[256]{0:T(256)}, u32[]{:S(2)}) copy-start(s32[256]{0:T(256)} %param.18) | copy-start | bytes 3076
  40.5 0.8 copy-start.2
  41.3 16.3 %all-to-all-start.1 = ((bf16[16,72,256]{2,1,0:T(8,128)(2,1)}), bf16[16,72,256]{2,1,0:T(8,128)(2,1)S(1)}, u32[]{:S(2)}, u32[]{:S(2)}) async-start(bf16[16,72,256]{2,1,0:T(8,128)(2,1)} %copy-done.2), calls=%async_computation.1 | async-start | bytes 1179648 | tf_op jit(solution)/shard_map/all_to_all | solution.py:290
  45.6 1.1 copy-start.1
  46.7 1.1 copy-start.8
  47.8 1.6 %copy-start.10 = (bf16[512,2048]{1,0:T(8,128)(2,1)S(1)}, bf16[512,2048]{1,0:T(8,128)(2,1)}, u32[]{:S(2)}) copy-start(bf16[512,2048]{1,0:T(8,128)(2,1)} %constant.43.clone.high_ref) | copy-start | bytes 6291460
  49.4 8.2 %copy-start.6 = (s32[16,1]{0,1:T(1,128)S(1)}, s32[16,1]{0,1:T(1,128)}, u32[]{:S(2)}) copy-start(s32[16,1]{0,1:T(1,128)} %param.20) | copy-start | bytes 196
  49.4 8.2 %copy-start.7 = (s32[16]{0:T(128)S(1)}, s32[16]{0:T(128)}, u32[]{:S(2)}) copy-start(s32[16]{0:T(128)} %cloudy_ref.1) | copy-start | bytes 196
  59.6 0.7 copy-start.3
  60.3 26.5 %all-to-all-start.2 = ((bf16[256,4,128]{2,1,0:T(4,128)(2,1)}), bf16[256,4,128]{2,1,0:T(4,128)(2,1)S(1)}, u32[]{:S(2)}, u32[]{:S(2)}) async-start(bf16[256,4,128]{2,1,0:T(4,128)(2,1)} %bitcast.46), calls=%async_computation.2 | async-start | bytes 524288 | tf_op jit(solution)/shard_map/all_to_all | solution.py:317

commit v2 on v1

v2 whole, which is shorter than its diff:
```python
import functools
import math

import jax
import jax.numpy as jnp
import numpy as np
from jax import lax
from jax.experimental import pallas as pl
from jax.experimental.pallas import tpu as pltpu
from jax.sharding import PartitionSpec as P

NB_ROW = 16
CMAX = 128
CAP = 2
LANES = 128
TIME_STEP = 0.5
ORDER = ("phys", "dyn")
VMEM = pl.BlockSpec(memory_space=pltpu.VMEM)
SMEM = pl.BlockSpec(memory_space=pltpu.SMEM)
HBM = pl.BlockSpec(memory_space=pltpu.HBM)
BF16 = jnp.bfloat16
F32 = jnp.float32


def params(mebibytes=32):
    return pltpu.CompilerParams(vmem_limit_bytes=mebibytes << 20)


def in_hbm(*arrays):
    return [pltpu.with_memory_space_constraint(array, pltpu.HBM) for array in arrays]


def wave_table(waves, n_lon):
    phases = np.arange(waves)[:, None] * np.arange(n_lon)[None, :] % n_lon
    angles = phases.astype(np.float64) * (2.0 * math.pi / n_lon)
    table = np.concatenate([np.cos(angles), -np.sin(angles)], axis=0).astype(np.float32)
    high = table.astype(jnp.bfloat16)
    low = (table - high.astype(np.float32)).astype(jnp.bfloat16)
    return high, low


def dot(a, b):
    return jnp.dot(a, b, preferred_element_type=F32)


def dot_nt(a, b):
    return lax.dot_general(a, b, (((1,), (1,)), ((), ())), preferred_element_type=F32)


def dot_tn(a, b):
    return lax.dot_general(a, b, (((0,), (0,)), ((), ())), preferred_element_type=F32)


def split(value):
    high = value.astype(BF16)
    return high, (value - high.astype(F32)).astype(BF16)


def place_kernel(
    expert_hbm, state_hbm, legendre_hbm, out_ref, expert_ref, state_ref, legendre_ref, count_ref, sems
):
    networks, _, width = out_ref.shape
    blocks, levels, _ = state_ref.shape
    share = legendre_ref.shape[1] // CAP
    fetches = [
        pltpu.make_async_copy(state_hbm.at[:, block, :], state_ref.at[block], sems.at[block])
        for block in range(blocks)
    ]
    expert_fetch = pltpu.make_async_copy(expert_hbm, expert_ref, sems.at[blocks])
    legendre_fetch = pltpu.make_async_copy(legendre_hbm, legendre_ref, sems.at[blocks + 1])
    expert_fetch.start()
    legendre_fetch.start()
    for fetch in fetches:
        fetch.start()
    out_ref[:, share:, :] = jnp.zeros((networks, levels, width), BF16)
    for network in range(networks):
        count_ref[network] = 0
    expert_fetch.wait()
    legendre_fetch.wait()
    for network in range(networks):
        for half in range(CAP):
            part = legendre_ref[network, pl.ds(half, share, stride=CAP), :]
            out_ref[network, :share, half * CMAX : (half + 1) * CMAX] = part.astype(BF16)
    for block in range(blocks):
        network = expert_ref[block]
        rank = count_ref[network]
        count_ref[network] = rank + 1
        lanes = pl.ds(pl.multiple_of(rank * CMAX, CMAX), CMAX)
        fetches[block].wait()
        out_ref[network, share:, lanes] = (0.5 * state_ref[block]).astype(BF16)


def place_blocks(experts, state, legendre):
    levels, blocks, width = state.shape
    networks, share, _ = legendre.shape
    return pl.pallas_call(
        place_kernel,
        in_specs=[HBM] * 3,
        out_specs=VMEM,
        out_shape=pltpu.HBM((networks, share // CAP + levels, CAP * CMAX), BF16),
        scratch_shapes=[
            pltpu.SMEM((blocks,), jnp.int32),
            pltpu.VMEM((blocks, levels, width), F32),
            pltpu.VMEM(legendre.shape, F32),
            pltpu.SMEM((networks,), jnp.int32),
            pltpu.SemaphoreType.DMA((blocks + 2,)),
        ],
        compiler_params=params(),
        name="place",
    )(*in_hbm(experts, state, legendre))


def prepare_kernel(
    n_lon, order_ref, state_hbm, prev_hbm, high_hbm, low_hbm, in_hbm, mid_hbm, last_hbm,
    table_ref, out_ref, first_ref, middle_ref, last_ref,
    state_ref, prev_ref, high_ref, low_ref, in_ref, mid_ref, sems
):
    levels, blocks, _ = state_ref.shape
    waves = order_ref.shape[0]
    pairs = (
        (mid_hbm, mid_ref), (in_hbm, in_ref), (last_hbm, last_ref),
        (high_hbm, high_ref), (state_hbm, state_ref), (prev_hbm, prev_ref), (low_hbm, low_ref),
    )
    fetches = [
        pltpu.make_async_copy(source, target, sems.at[i]) for i, (source, target) in enumerate(pairs)
    ]
    for fetch in fetches:
        fetch.start()
    for fetch in fetches[:4]:
        fetch.wait()
    side = waves
    diagonal = lax.broadcasted_iota(jnp.int32, (side, side), 0) == lax.broadcasted_iota(
        jnp.int32, (side, side), 1
    )
    half = jnp.where(diagonal, 0.5, 0.0).astype(BF16)
    for start in range(0, mid_ref.shape[1], side):
        rows = slice(start, start + side)
        middle_ref[rows, :] = dot_nt(half, mid_ref[:, rows]).astype(BF16)
        first_ref[rows, :] = (2.0 * dot_nt(half, in_ref[:, rows])).astype(BF16)
    for part in range(2):
        rows = slice(part * waves, (part + 1) * waves)
        table_ref[rows, :] = dot(order_ref[...], high_ref[rows, :]).astype(BF16)
    for fetch in fetches[4:]:
        fetch.wait()
    parts = [
        state_ref[:, block, :] + TIME_STEP * prev_ref[:, block, :] for block in range(blocks)
    ]
    forcing = jnp.concatenate(parts, axis=1)
    blank = jnp.zeros((LANES - levels, n_lon), F32)
    high, low = split(jnp.concatenate([forcing, blank], axis=0))
    both = dot_nt(high_ref[...], jnp.concatenate([high, low], axis=0))
    natural = both[:, :LANES] + (both[:, LANES:] + dot_nt(low_ref[...], high))
    natural = (natural * (1.0 / math.sqrt(n_lon))).astype(BF16)
    for part in range(2):
        rows = slice(part * waves, (part + 1) * waves)
        out_ref[rows, :] = dot(order_ref[...], natural[rows, :]).astype(BF16)


def prepare(state, prev, order, high, low, w_in, w_mid, w_out):
    rows, n_lon = high.shape
    levels, hidden = w_in.shape
    return pl.pallas_call(
        functools.partial(prepare_kernel, n_lon),
        in_specs=[VMEM] + [HBM] * 7,
        out_specs=[VMEM] * 5,
        out_shape=[
            pltpu.HBM((rows, n_lon), BF16),
            pltpu.HBM((rows, LANES), BF16),
            jax.ShapeDtypeStruct((hidden, levels), BF16),
            jax.ShapeDtypeStruct((hidden, hidden), BF16),
            jax.ShapeDtypeStruct((levels, hidden), BF16),
        ],
        scratch_shapes=[
            pltpu.VMEM(state.shape, F32),
            pltpu.VMEM(prev.shape, F32),
            pltpu.VMEM(high.shape, BF16),
            pltpu.VMEM(low.shape, BF16),
            pltpu.VMEM(w_in.shape, BF16),
            pltpu.VMEM(w_mid.shape, BF16),
            pltpu.SemaphoreType.DMA((7,)),
        ],
        compiler_params=params(),
        cost_estimate=pl.CostEstimate(
            flops=4 * rows * n_lon * rows, bytes_accessed=12 << 20, transcendentals=0
        ),
        name="prepare",
    )(order, *in_hbm(state, prev, high, low, w_in, w_mid, w_out))


def silu(half):
    return (half + half * jnp.tanh(half)).astype(BF16)


def network_kernel(skip, group, x_ref, first_ref, middle_ref, last_ref, out_ref, own_ref):
    width = x_ref.shape[2]
    own_ref[...] = x_ref[:, :skip, :]
    for start in range(0, x_ref.shape[0], group):
        columns = jnp.concatenate([x_ref[start + i, skip:, :] for i in range(group)], axis=1)
        one = silu(dot(first_ref[...], columns))
        two = silu(dot(middle_ref[...], one))
        out = dot(last_ref[...], two).astype(BF16)
        for i in range(group):
            out_ref[start + i] = out[:, i * width : (i + 1) * width]


def network(arrived, first_w, middle_w, last_w):
    senders, rows, width = arrived.shape
    levels, hidden = last_w.shape
    step = 4
    return pl.pallas_call(
        functools.partial(network_kernel, rows - levels, 2),
        grid=(senders // step,),
        in_specs=[
            pl.BlockSpec((step, rows, width), lambda i: (i, 0, 0)),
            pl.BlockSpec((hidden, levels), lambda i: (0, 0)),
            pl.BlockSpec((hidden, hidden), lambda i: (0, 0)),
            pl.BlockSpec((levels, hidden), lambda i: (0, 0)),
        ],
        out_specs=[
            pl.BlockSpec((step, levels, width), lambda i: (i, 0, 0)),
            pl.BlockSpec((step, rows - levels, width), lambda i: (i, 0, 0)),
        ],
        out_shape=[
            jax.ShapeDtypeStruct((senders, levels, width), BF16),
            pltpu.HBM((senders, rows - levels, width), BF16),
        ],
        compiler_params=params(),
        cost_estimate=pl.CostEstimate(
            flops=2 * senders * width * hidden * (hidden + 2 * 256),
            bytes_accessed=4 << 20,
            transcendentals=2 * senders * width * hidden,
        ),
        name="network",
    )(arrived, first_w, middle_w, last_w)


def return_kernel(
    n_lon, returned_ref, expert_hbm, cloudy_hbm, table_hbm, first_hbm, tend_ref, out_ref,
    expert_ref, cloudy_ref, table_ref, first_ref, count_ref, rows_ref, sems
):
    networks, levels, _ = returned_ref.shape
    waves = first_ref.shape[0] // 2
    pairs = (
        (expert_hbm, expert_ref), (cloudy_hbm, cloudy_ref), (table_hbm, table_ref), (first_hbm, first_ref),
    )
    fetches = [
        pltpu.make_async_copy(source, target, sems.at[i]) for i, (source, target) in enumerate(pairs)
    ]
    for fetch in fetches:
        fetch.start()
    lanes = lax.broadcasted_iota(jnp.int32, (levels, CMAX), 1)
    for network in range(networks):
        count_ref[network] = 0
    for fetch in fetches[:2]:
        fetch.wait()
    for block in range(NB_ROW):
        network = expert_ref[block]
        rank = count_ref[network]
        count_ref[network] = rank + 1
        place = pl.ds(pl.multiple_of(rank * CMAX, CMAX), CMAX)
        values = returned_ref[network, :, place].astype(F32)
        kept = jnp.where(lanes < cloudy_ref[block], values, 0.0)
        tend_ref[:, block * CMAX : (block + 1) * CMAX] = kept.astype(BF16)
    for fetch in fetches[2:]:
        fetch.wait()
    out = dot_nt(table_ref[...], tend_ref[...]) * (TIME_STEP / math.sqrt(n_lon))
    out = jnp.concatenate([out, jnp.zeros((out.shape[0], LANES - levels), F32)], axis=1)
    for part in range(2):
        rows = slice(part * waves, (part + 1) * waves)
        rows_ref[pl.ds(part, waves, stride=4), :] = first_ref[rows, :].astype(F32)
        rows_ref[pl.ds(2 + part, waves, stride=4), :] = out[rows]
    out_ref[...] = rows_ref[...].astype(BF16)


def return_blocks(returned, experts, cloudy, table, first):
    rows, n_lon = table.shape
    networks, levels, _ = returned.shape
    return pl.pallas_call(
        functools.partial(return_kernel, n_lon),
        in_specs=[VMEM] + [HBM] * 4,
        out_specs=[VMEM] * 2,
        out_shape=[
            pltpu.HBM((levels, n_lon), BF16),
            jax.ShapeDtypeStruct((2 * rows, LANES), BF16),
        ],
        scratch_shapes=[
            pltpu.SMEM(experts.shape, jnp.int32),
            pltpu.SMEM(cloudy.shape, jnp.int32),
            pltpu.VMEM(table.shape, BF16),
            pltpu.VMEM(first.shape, BF16),
            pltpu.SMEM((networks,), jnp.int32),
            pltpu.VMEM((2 * rows, LANES), F32),
            pltpu.SemaphoreType.DMA((4,)),
        ],
        compiler_params=params(),
        name="return",
    )(returned, *in_hbm(experts, cloudy, table, first))


def solve_kernel(
    scale, again, me_ref, got_ref, wave_hbm, own_hbm, analysis_hbm, rate_hbm, out_ref,
    wave_ref, own_ref, analysis_ref, rate_ref, rows_ref, turn_ref, sems
):
    levels = analysis_ref.shape[0]
    networks, share, coeffs = own_ref.shape
    lats = networks * share
    pairs = (
        (wave_hbm, wave_ref), (own_hbm, own_ref), (analysis_hbm, analysis_ref), (rate_hbm, rate_ref),
    )
    fetches = [
        pltpu.make_async_copy(source, target, sems.at[i]) for i, (source, target) in enumerate(pairs)
    ]
    for fetch in fetches:
        fetch.start()
    rows_ref[...] = got_ref[...].astype(F32)
    parts = [rows_ref[pl.ds(part, lats, stride=4), :].astype(BF16) for part in range(4)]
    for fetch in fetches:
        fetch.wait()
    table = jnp.concatenate([own_ref[sender] for sender in range(networks)], axis=0)

    wave = wave_ref[me_ref[0]]
    total = (wave + lax.broadcasted_iota(jnp.int32, (levels, coeffs), 1)).astype(F32)
    rate = jnp.concatenate([rate_ref[...], jnp.zeros((1, LANES - levels), F32)], axis=1)
    rate = jnp.broadcast_to(rate, (LANES, LANES)).T[:levels]
    rate = jnp.concatenate([rate, rate], axis=1)
    inverse = 1.0 / (1.0 + TIME_STEP * (total * (total + 1.0) * scale + rate))
    blank = jnp.zeros((LANES - levels, coeffs), F32)
    gains, pulls = [], []
    for part in range(2):
        halves = [analysis_ref[:, 2 * part + half, :] for half in range(2)]
        pulled = TIME_STEP * rate * jnp.concatenate(halves, axis=1) * inverse
        gains += [inverse * (1.0 / lats), blank]
        pulls += [pulled * (1.0 / math.sqrt(coeffs)), blank]
    gain = jnp.concatenate(gains, axis=0)
    pull = jnp.concatenate(pulls, axis=0)
    real = jnp.where(wave == 0, 2.0 * again, again)
    imag = jnp.where(wave == 0, 0.0, again)
    lane = lax.broadcasted_iota(jnp.int32, (1, 2 * LANES), 1)
    regain = jnp.where(lane < LANES, real, imag)

    def there(value):
        both = dot_tn(jnp.concatenate(split(value), axis=1), table)
        return both[: 2 * LANES] + both[2 * LANES :]

    def back(value):
        both = dot_nt(table, jnp.concatenate(split(value), axis=0))
        return both[:, : 2 * LANES] + both[:, 2 * LANES :]

    spectral = dot_tn(jnp.concatenate(parts, axis=1), table)
    first = back(spectral[: 2 * LANES] * gain + pull)
    second = spectral[2 * LANES :] + there(first * regain)
    final = back(second * gain + pull)
    for part in range(2):
        turn_ref[pl.ds(part, lats, stride=2), :] = final[:, part * LANES : (part + 1) * LANES]
    out_ref[...] = turn_ref[...].astype(BF16)


def solve_twice(scale, again, me, got, waves, own, analysis, rate):
    rows = got.shape[0]
    return pl.pallas_call(
        functools.partial(solve_kernel, scale, again),
        in_specs=[SMEM, VMEM] + [HBM] * 4,
        out_specs=VMEM,
        out_shape=jax.ShapeDtypeStruct((rows // 2, LANES), BF16),
        scratch_shapes=[
            pltpu.SMEM(waves.shape, jnp.int32),
            pltpu.VMEM(own.shape, BF16),
            pltpu.VMEM(analysis.shape, F32),
            pltpu.VMEM(rate.shape, F32),
            pltpu.VMEM((rows, LANES), F32),
            pltpu.VMEM((rows // 2, LANES), F32),
            pltpu.SemaphoreType.DMA((4,)),
        ],
        compiler_params=params(),
        name="solve",
    )(me, got, *in_hbm(waves, own, analysis, rate))


def synthesis_kernel(scale, home_ref, table_ref, out_ref, rows_ref):
    levels, blocks, width = out_ref.shape
    waves = home_ref.shape[0] // 2
    rows_ref[...] = home_ref[...].astype(F32)
    parts = [rows_ref[pl.ds(part, waves, stride=2), :].astype(BF16) for part in range(2)]
    grid = dot_tn(jnp.concatenate(parts, axis=0), table_ref[...]) * scale
    for block in range(blocks):
        out_ref[:, block, :] = grid[:levels, block * width : (block + 1) * width]


def synthesis(home, table, levels, scale):
    n_lon = table.shape[1]
    return pl.pallas_call(
        functools.partial(synthesis_kernel, scale),
        in_specs=[VMEM] * 2,
        out_specs=VMEM,
        out_shape=jax.ShapeDtypeStruct((levels, NB_ROW, n_lon // NB_ROW), F32),
        scratch_shapes=[pltpu.VMEM(home.shape, F32)],
        compiler_params=params(),
        name="synthesis",
    )(home, table)


def on_device(
    initial_state,
    prev_tendency,
    analysis,
    legendre,
    nudge_rate,
    band_waves,
    cloudy_count,
    expert_of,
    w_in,
    w_mid,
    w_out,
):
    levels, _, n_lon = initial_state.shape
    n_dyn = lax.axis_size("dyn")
    n_phys = lax.axis_size("phys")
    waves = band_waves.shape[0]
    coeffs = legendre.shape[3]
    lats = waves
    rows = 2 * waves
    state = initial_state.reshape(levels, NB_ROW, n_lon // NB_ROW)
    prev = prev_tendency.reshape(levels, NB_ROW, n_lon // NB_ROW)
    experts = expert_of[:, 0]

    share = lats // n_phys

    outgoing = place_blocks(experts, state, legendre.reshape(n_phys, share * CAP, coeffs // CAP))
    arrived = lax.all_to_all(outgoing, "phys", split_axis=0, concat_axis=0, tiled=True)

    high, low = (jnp.asarray(part) for part in wave_table(waves, n_lon))
    chunk_waves = band_waves.reshape(n_dyn, n_phys).T.reshape(waves, 1)
    order = (chunk_waves == jnp.arange(waves, dtype=jnp.int32)[None, :]).astype(BF16)
    table, first, first_w, middle_w, last_w = prepare(
        state, prev, order, high, low, w_in[0], w_mid[0], w_out[0]
    )
    me = lax.axis_index("dyn") * n_phys + lax.axis_index("phys")
    arrived, table, first, first_w, middle_w, last_w = lax.optimization_barrier(
        (arrived, table, first, first_w, middle_w, last_w)
    )
    computed, own = network(arrived, first_w, middle_w, last_w)
    returned = lax.all_to_all(computed, "phys", split_axis=0, concat_axis=0, tiled=True)

    tendency, sent = return_blocks(returned, experts, cloudy_count, table, first)
    got = lax.all_to_all(
        sent.reshape(waves, 4, LANES), ORDER, split_axis=0, concat_axis=0, tiled=True
    )
    back = solve_twice(
        1.0 / (waves * (waves + 1.0)),
        (n_lon / 2.0) / math.sqrt(waves) / math.sqrt(n_lon),
        me.reshape(1),
        got.reshape(4 * lats, LANES),
        band_waves,
        own,
        analysis.reshape(levels, 2 * coeffs // LANES, LANES),
        nudge_rate[None, :],
    )
    home = lax.all_to_all(
        back.reshape(lats, 2, LANES), ORDER, split_axis=0, concat_axis=0, tiled=True
    )
    final = synthesis(home.reshape(rows, LANES), table, levels, 1.0 / math.sqrt(waves))
    return (final.reshape(levels, 1, n_lon), tendency.reshape(levels, 1, n_lon))


def solution(mesh):
    in_specs = (
        P(None, ("dyn", "phys"), None),
        P(None, ("dyn", "phys"), None),
        P(None, None, ("dyn", "phys"), None),
        P("dyn", None, "phys", None),
        P(),
        P(),
        P(("dyn", "phys")),
        P(("dyn", "phys"), None),
        P("phys", None, None),
        P("phys", None, None),
        P("phys", None, None),
    )
    out_specs = (P(None, ("dyn", "phys"), None), P(None, ("dyn", "phys"), None))
    return jax.shard_map(
        on_device, mesh=mesh, in_specs=in_specs, out_specs=out_specs, check_vma=False
    )
```

time: 109 us -> 106 us (0.972)
  blocking collectives: 18.5 us -> 34.5 us
  local copies, waits for them, and re-layouts: 13.4 us -> 0.24 us
  Pallas kernels: 23.1 us -> 28.9 us
  starting transfers between devices: 23.7 us -> 18.8 us
  other arithmetic: 3.72 us -> 0.11 us
  waiting for transfers between devices: 24 us -> 22.6 us
    all_to_all x1 -> x2, blocking collectives: 18.5 us -> 34.5 us  [the longest x1 18.4 us: on_device(): lax.all_to_all(back.reshape(lats, 2, LANES), ORDER, split_axis=0, concat_...]
    unnamed x32 -> x4, local copies, waits for them, and re-layouts: 10.7 us -> 0.01 us
    pallas_call x4, Pallas kernels: 8.65 us -> 14 us  [the longest x1 6.58 us: prepare(): pl.pallas_call(functools.partial(prepare_kernel, n_lon), in_specs=[VMEM]...]
    all_to_all x2 -> x1, starting transfers between devices: 15.3 us -> 10.3 us  [on_device(): lax.all_to_all(sent.reshape(waves, 4, LANES), ORDER, split_axis=0, concat...]
    all_to_all x1, waiting for transfers between devices: 9.08 us -> 6.75 us  [on_device(): lax.all_to_all(outgoing, 'phys', split_axis=0, concat_axis=0, tiled=True)]
    transpose x2 -> x0, other arithmetic: 1.83 us -> none  [the longest x1 1.81 us: on_device(): middle_w = (w_mid[0] * 0.5).T]
    mul x2 -> x0, other arithmetic: 1.71 us -> none  [the longest x1 1.08 us: on_device(): pull = pulled * (1.0 / math.sqrt(coeffs))]
    transpose x4 -> x1, local copies, waits for them, and re-layouts: 1.21 us -> 0.07 us  [on_device(): chunk_waves = band_waves.reshape(n_dyn, n_phys).T.reshape(waves, 1)]
  transfers between devices with their start and end apart: 3 -> 2, of which waited for: 3 -> 2; matrix products, arithmetic and copies ran while one was open for 8% -> 0% of each run, Pallas kernels for 3% -> 6%
where the time goes in v2:
time: 106 us
  blocking collectives  34.5 us (33%)
  Pallas kernels  28.9 us (27%)
  waiting for transfers between devices  22.6 us (21%)
  starting transfers between devices  18.8 us (18%)
    all_to_all x1, blocking collectives, on_device(): lax.all_to_all(back.reshape(lats, 2, LANES), ORDER, split_axis=0, concat_...  18.4 us
    all_to_all x1, blocking collectives, on_device(): lax.all_to_all(computed, 'phys', split_axis=0, concat_axis=0, tiled=True)  16.1 us
    all_to_all x1, waiting for transfers between devices, on_device(): lax.all_to_all(sent.reshape(waves, 4, LANES), ORDER, split_axis=0, concat...  15.8 us
    pallas_call x1, Pallas kernels, network(): pl.pallas_call(functools.partial(network_kernel, rows - levels, 2), grid=...  13.4 us
    all_to_all x1, starting transfers between devices, on_device(): lax.all_to_all(sent.reshape(waves, 4, LANES), ORDER, split_axis=0, concat...  10.3 us
    all_to_all x1, starting transfers between devices, on_device(): lax.all_to_all(outgoing, 'phys', split_axis=0, concat_axis=0, tiled=True)  8.46 us
    all_to_all x1, waiting for transfers between devices, on_device(): lax.all_to_all(outgoing, 'phys', split_axis=0, concat_axis=0, tiled=True)  6.75 us
    pallas_call x1, Pallas kernels, prepare(): pl.pallas_call(functools.partial(prepare_kernel, n_lon), in_specs=[VMEM]...  6.58 us
  transfers between devices with their start and end apart: 2, of which 2 were waited for; matrix products, arithmetic and copies ran while one was open for 0% of the time, Pallas kernels for 6%

profile of v2, /device:TPU:1, one launch (start us, length us, event | category | flops | bytes accessed | tf_op | source)
XLA Modules:
  0.0 105.8 jit_solution(15937018437221121745)
XLA Ops:
  0.6 0.0 copy-start.1
  0.6 2.2 %place.1 = bf16[16,88,256]{2,1,0:T(8,128)(2,1)} custom-call(s32[16]{0:T(128)} %bitcast.26, f32[72,16,128]{2,1,0:T(8,128)} %bitcast.20, f32[16,32,128]{2,1,0:T(8,128)} %bitcast.23), custom_call_target="tpu_custom_call" | custom-call | tf_op jit(solution)/shard_map/place/pallas_call | solution.py:96
  2.8 8.5 %all-to-all-start = ((bf16[16,88,256]{2,1,0:T(8,128)(2,1)}), bf16[16,88,256]{2,1,0:T(8,128)(2,1)S(1)}, u32[]{:S(2)}, u32[]{:S(2)}) async-start(bf16[16,88,256]{2,1,0:T(8,128)(2,1)} %place.1), calls=%async_computation | async-start | bytes 1441792 | tf_op jit(solution)/shard_map/all_to_all | solution.py:429
  11.3 0.0 copy-done.1
  11.3 0.1 reshape.45
  11.4 0.1 copy.17
  11.4 0.1 eq.15
  11.5 0.1 fusion.order_ref
  11.6 6.6 %prepare.1 = (bf16[512,2048]{1,0:T(8,128)(2,1)}, bf16[512,128]{1,0:T(8,128)(2,1)}, bf16[1024,72]{1,0:T(8,128)(2,1)S(1)}, bf16[1024,1024]{1,0:T(8,128)(2,1)S(1)}, bf16[72,1024]{1,0:T(8,128)(2,1)S(1)}) custom-call(bf16[256,256]{1,0:T(8,128)(2,1)S(1)} %fusion.order_ref, f32[72,16,128]{2,1,0:T(8,128)} %bitcast.21, f32[72,16,128]{2,1,0:T(8,128)} %bitcast.30, ...), custom_call_target="tpu_custom_call" | custom-call | flops 2147483648 | bytes 12582912 | tf_op jit(solution)/shard_map/prepare/pallas_call | solution.py:162
  18.2 6.7 %all-to-all-done.x_ref = bf16[16,88,256]{2,1,0:T(8,128)(2,1)S(1)} async-done(((bf16[16,88,256]{2,1,0:T(8,128)(2,1)}), bf16[16,88,256]{2,1,0:T(8,128)(2,1)S(1)}, u32[]{:S(2)}, u32[]{:S(2)}) %all-to-all-start) | async-done | bytes 720928 | tf_op jit(solution)/shard_map/all_to_all | solution.py:429
  25.0 13.4 %network.1 = (bf16[16,72,256]{2,1,0:T(8,128)(2,1)S(1)}, bf16[16,16,256]{2,1,0:T(8,128)(2,1)}) custom-call(bf16[16,88,256]{2,1,0:T(8,128)(2,1)S(1)} %all-to-all-done.x_ref, bf16[1024,72]{1,0:T(8,128)(2,1)S(1)} %get-tuple-element.23.first_ref, bf16[1024,1024]{1,0:T(8,128)(2,1)S(1)} %get-tuple-element.24.middle_ref, bf16[72,1024]{1,0:T(8,128)(2,1)S(1)} %get-tuple-element.25.last_ref), custom_call_target="tpu_custom_call" | custom-call | flops 12884901888 | bytes 4194304 | tf_op jit(solution)/shard_map/network/pallas_call | solution.py:210
  38.4 16.1 %all_to_all.20.returned_ref = bf16[16,72,256]{2,1,0:T(8,128)(2,1)S(1)} all-to-all(bf16[16,72,256]{2,1,0:T(8,128)(2,1)S(1)} %get-tuple-element.26), channel_id=1, replica_groups=mesh['dyn'=16,'phys'=16] {'phys'}, dimensions={0} | all-to-all | bytes 1179648 | tf_op jit(solution)/shard_map/all_to_all | solution.py:442
  54.5 0.0 copy-start
  54.5 3.2 %return.1 = (bf16[72,2048]{1,0:T(8,128)(2,1)}, bf16[1024,128]{1,0:T(8,128)(2,1)}) custom-call(bf16[16,72,256]{2,1,0:T(8,128)(2,1)S(1)} %all_to_all.20.returned_ref, s32[16]{0:T(128)} %bitcast.27, s32[16]{0:T(128)} %cloudy_hbm.1, bf16[512,2048]{1,0:T(8,128)(2,1)} %get-tuple-element.27.table_hbm.table_ref, bf16[512,128]{1,0:T(8,128)(2,1)} %get-tuple-element.28.first_hbm), custom_call_target="tpu_custom_call" | custom-call | tf_op jit(solution)/shard_map/return/pallas_call | solution.py:278
  57.7 10.3 %all-to-all-start.2 = ((bf16[256,4,128]{2,1,0:T(4,128)(2,1)}), bf16[256,4,128]{2,1,0:T(4,128)(2,1)S(1)}, u32[]{:S(2)}, u32[]{:S(2)}) async-start(bf16[256,4,128]{2,1,0:T(4,128)(2,1)} %bitcast.9), calls=%async_computation.2 | async-start | bytes 524288 | tf_op jit(solution)/shard_map/all_to_all | solution.py:445
  68.1 15.8 %all-to-all-done.2 = bf16[256,4,128]{2,1,0:T(4,128)(2,1)S(1)} async-done(((bf16[256,4,128]{2,1,0:T(4,128)(2,1)}), bf16[256,4,128]{2,1,0:T(4,128)(2,1)S(1)}, u32[]{:S(2)}, u32[]{:S(2)}) %all-to-all-start.2) | async-done | bytes 262176 | tf_op jit(solution)/shard_map/all_to_all | solution.py:445
  83.9 2.1 %solve.1 = bf16[512,128]{1,0:T(8,128)(2,1)S(1)} custom-call(s32[1]{0:T(128)} %bitcast.me_ref, bf16[1024,128]{1,0:T(8,128)(2,1)S(1)} %bitcast.17, s32[256]{0:T(256)} %wave_hbm.1, bf16[16,16,256]{2,1,0:T(8,128)(2,1)} %get-tuple-element.30.own_hbm, f32[72,4,128]{2,1,0:T(4,128)} %bitcast.24, f32[1,72]{1,0:T(1,128)} %bitcast.28), custom_call_target="tpu_custom_call" | custom-call | tf_op jit(solution)/shard_map/solve/pallas_call | solution.py:360
  86.0 18.4 %all_to_all.21 = bf16[256,2,128]{2,1,0:T(2,128)(2,1)S(1)} all-to-all(bf16[256,2,128]{2,1,0:T(2,128)(2,1)S(1)} %bitcast.19), channel_id=1, replica_groups=mesh['dyn'=16,'phys'=16] {'phys','dyn'}, dimensions={0} | all-to-all | bytes 262144 | tf_op jit(solution)/shard_map/all_to_all | solution.py:458
  104.3 0.0 copy-done
  104.3 1.5 %synthesis.1 = f32[72,16,128]{2,1,0:T(8,128)} custom-call(bf16[512,128]{1,0:T(8,128)(2,1)S(1)} %bitcast.18, bf16[512,2048]{1,0:T(8,128)(2,1)S(1)} %copy-done), custom_call_target="tpu_custom_call" | custom-call | tf_op jit(solution)/shard_map/synthesis/pallas_call | solution.py:391
Async XLA Ops:
  0.6 10.6 %copy-start.1 = (s32[256]{0:T(256)S(1)}, s32[256]{0:T(256)}, u32[]{:S(2)}) copy-start(s32[256]{0:T(256)} %wave_hbm.1) | copy-start | bytes 3076
  2.8 22.2 %all-to-all-start = ((bf16[16,88,256]{2,1,0:T(8,128)(2,1)}), bf16[16,88,256]{2,1,0:T(8,128)(2,1)S(1)}, u32[]{:S(2)}, u32[]{:S(2)}) async-start(bf16[16,88,256]{2,1,0:T(8,128)(2,1)} %place.1), calls=%async_computation | async-start | bytes 1441792 | tf_op jit(solution)/shard_map/all_to_all | solution.py:429
  54.5 49.8 %copy-start = (bf16[512,2048]{1,0:T(8,128)(2,1)S(1)}, bf16[512,2048]{1,0:T(8,128)(2,1)}, u32[]{:S(2)}) copy-start(bf16[512,2048]{1,0:T(8,128)(2,1)} %get-tuple-element.27.table_hbm.table_ref) | copy-start | bytes 6291460
  57.7 26.2 %all-to-all-start.2 = ((bf16[256,4,128]{2,1,0:T(4,128)(2,1)}), bf16[256,4,128]{2,1,0:T(4,128)(2,1)S(1)}, u32[]{:S(2)}, u32[]{:S(2)}) async-start(bf16[256,4,128]{2,1,0:T(4,128)(2,1)} %bitcast.9), calls=%async_computation.2 | async-start | bytes 524288 | tf_op jit(solution)/shard_map/all_to_all | solution.py:445

commit v3 on v2

--- a/solution.py
+++ b/solution.py
@@ -13,6 +13,8 @@
 CMAX = 128
 CAP = 2
 LANES = 128
+MARK = 1e30
+GROUP = 512
 TIME_STEP = 0.5
 ORDER = ("phys", "dyn")
 VMEM = pl.BlockSpec(memory_space=pltpu.VMEM)
@@ -57,7 +59,8 @@
 
 
 def place_kernel(
-    expert_hbm, state_hbm, legendre_hbm, out_ref, expert_ref, state_ref, legendre_ref, count_ref, sems
+    expert_hbm, cloudy_hbm, state_hbm, legendre_hbm, out_ref,
+    expert_ref, cloudy_ref, state_ref, legendre_ref, chunk_ref, used_ref, sems
 ):
     networks, _, width = out_ref.shape
     blocks, levels, _ = state_ref.shape
@@ -66,48 +69,60 @@
         pltpu.make_async_copy(state_hbm.at[:, block, :], state_ref.at[block], sems.at[block])
         for block in range(blocks)
     ]
-    expert_fetch = pltpu.make_async_copy(expert_hbm, expert_ref, sems.at[blocks])
-    legendre_fetch = pltpu.make_async_copy(legendre_hbm, legendre_ref, sems.at[blocks + 1])
-    expert_fetch.start()
-    legendre_fetch.start()
-    for fetch in fetches:
+    pairs = ((expert_hbm, expert_ref), (cloudy_hbm, cloudy_ref), (legendre_hbm, legendre_ref))
+    early = [
+        pltpu.make_async_copy(source, target, sems.at[blocks + i])
+        for i, (source, target) in enumerate(pairs)
+    ]
+    for fetch in early + fetches:
         fetch.start()
-    out_ref[:, share:, :] = jnp.zeros((networks, levels, width), BF16)
+    chunk_ref[...] = jnp.full((networks, levels, width), MARK, F32)
     for network in range(networks):
-        count_ref[network] = 0
-    expert_fetch.wait()
-    legendre_fetch.wait()
+        used_ref[network] = 0
+    for fetch in early:
+        fetch.wait()
     for network in range(networks):
         for half in range(CAP):
             part = legendre_ref[network, pl.ds(half, share, stride=CAP), :]
             out_ref[network, :share, half * CMAX : (half + 1) * CMAX] = part.astype(BF16)
+    lane = lax.broadcasted_iota(jnp.int32, (levels, CMAX), 1)
+    spans = []
     for block in range(blocks):
         network = expert_ref[block]
-        rank = count_ref[network]
-        count_ref[network] = rank + 1
-        lanes = pl.ds(pl.multiple_of(rank * CMAX, CMAX), CMAX)
-        fetches[block].wait()
-        out_ref[network, share:, lanes] = (0.5 * state_ref[block]).astype(BF16)
-
-
-def place_blocks(experts, state, legendre):
+        start = used_ref[network]
+        end = start + cloudy_ref[block]
+        used_ref[network] = end
+        spans.append((network, start, end))
+    for fetch in fetches:
+        fetch.wait()
+    for block, (network, start, end) in enumerate(spans):
+        turned = pltpu.roll(0.5 * state_ref[block], lax.rem(start, CMAX), 1)
+        here = (lane >= start) & (lane < end)
+        pltpu.store(chunk_ref.at[network, :, :CMAX], turned, mask=here)
+        pltpu.store(chunk_ref.at[network, :, CMAX:], turned, mask=lane + CMAX < end)
+    out_ref[:, share:, :] = chunk_ref[...].astype(BF16)
+
+
+def place_blocks(experts, cloudy, state, legendre):
     levels, blocks, width = state.shape
     networks, share, _ = legendre.shape
     return pl.pallas_call(
         place_kernel,
-        in_specs=[HBM] * 3,
+        in_specs=[HBM] * 4,
         out_specs=VMEM,
         out_shape=pltpu.HBM((networks, share // CAP + levels, CAP * CMAX), BF16),
         scratch_shapes=[
             pltpu.SMEM((blocks,), jnp.int32),
+            pltpu.SMEM((blocks,), jnp.int32),
             pltpu.VMEM((blocks, levels, width), F32),
             pltpu.VMEM(legendre.shape, F32),
+            pltpu.VMEM((networks, levels, CAP * CMAX), F32),
             pltpu.SMEM((networks,), jnp.int32),
-            pltpu.SemaphoreType.DMA((blocks + 2,)),
+            pltpu.SemaphoreType.DMA((blocks + 3,)),
         ],
         compiler_params=params(),
         name="place",
-    )(*in_hbm(experts, state, legendre))
+    )(*in_hbm(experts, cloudy, state, legendre))
 
 
 def prepare_kernel(
@@ -191,58 +206,96 @@
     return (half + half * jnp.tanh(half)).astype(BF16)
 
 
-def network_kernel(skip, group, x_ref, first_ref, middle_ref, last_ref, out_ref, own_ref):
-    width = x_ref.shape[2]
-    own_ref[...] = x_ref[:, :skip, :]
-    for start in range(0, x_ref.shape[0], group):
-        columns = jnp.concatenate([x_ref[start + i, skip:, :] for i in range(group)], axis=1)
-        one = silu(dot(first_ref[...], columns))
+def network_kernel(
+    x_ref, first_ref, middle_ref, last_ref, table_hbm, row_hbm, out_ref, own_ref, table_ref, row_ref,
+    packed_ref, done_ref, sems
+):
+    senders, levels, _ = out_ref.shape
+    share = x_ref.shape[1] - levels
+    fetches = [
+        pltpu.make_async_copy(table_hbm, table_ref, sems.at[0]),
+        pltpu.make_async_copy(row_hbm, row_ref, sems.at[1]),
+    ]
+    for fetch in fetches:
+        fetch.start()
+    own_ref[...] = x_ref[:, :share, :]
+    heads = [x_ref[sender, share : share + 16, :].astype(F32)[:1] for sender in range(senders)]
+    marked = jnp.where(jnp.concatenate(heads, axis=0) < 0.1 * MARK, 1.0, 0.0)
+    marked = marked[:, :CMAX] + marked[:, CMAX:]
+    lane = lax.broadcasted_iota(jnp.int32, (levels, CMAX), 1)
+
+    def tiles(start):
+        first = start // CMAX
+        return [pl.ds(pl.multiple_of((first + i) * CMAX, CMAX), CMAX) for i in range(3)]
+
+    starts = [jnp.int32(0)]
+    for sender in range(senders):
+        count = jnp.sum(marked[sender : sender + 1]).astype(jnp.int32)
+        starts.append(starts[-1] + count)
+    for sender in range(senders):
+        shift = lax.rem(starts[sender], CMAX)
+        places = tiles(starts[sender])
+        near = pltpu.roll(x_ref[sender, share:, :CMAX].astype(F32), shift, 1)
+        far = pltpu.roll(x_ref[sender, share:, CMAX:].astype(F32), shift, 1)
+        packed_ref[:, places[0]] = jnp.where(lane < shift, packed_ref[:, places[0]], near)
+        packed_ref[:, places[1]] = jnp.where(lane < shift, near, far)
+        packed_ref[:, places[2]] = far
+
+    def group(index, carry):
+        place = pl.ds(pl.multiple_of(index * GROUP, GROUP), GROUP)
+        one = silu(dot(first_ref[...], packed_ref[:, place].astype(BF16)))
         two = silu(dot(middle_ref[...], one))
-        out = dot(last_ref[...], two).astype(BF16)
-        for i in range(group):
-            out_ref[start + i] = out[:, i * width : (i + 1) * width]
-
-
-def network(arrived, first_w, middle_w, last_w):
+        done_ref[:, place] = dot(last_ref[...], two)
+        return carry
+
+    lax.fori_loop(0, (starts[-1] + (GROUP - 1)) // GROUP, group, 0)
+    for sender in range(senders):
+        shift = lax.rem(starts[sender], CMAX)
+        back = lax.rem(CMAX - shift, CMAX)
+        near, middle, far = (pltpu.roll(done_ref[:, place], back, 1) for place in tiles(starts[sender]))
+        keep = lane < CMAX - shift
+        out_ref[sender, :, :CMAX] = jnp.where(keep, near, middle).astype(BF16)
+        out_ref[sender, :, CMAX:] = jnp.where(keep, middle, far).astype(BF16)
+    for fetch in fetches:
+        fetch.wait()
+
+
+def network(arrived, first_w, middle_w, last_w, table, row):
     senders, rows, width = arrived.shape
     levels, hidden = last_w.shape
-    step = 4
+    columns = -(-senders * width // GROUP) * GROUP + GROUP
     return pl.pallas_call(
-        functools.partial(network_kernel, rows - levels, 2),
-        grid=(senders // step,),
-        in_specs=[
-            pl.BlockSpec((step, rows, width), lambda i: (i, 0, 0)),
-            pl.BlockSpec((hidden, levels), lambda i: (0, 0)),
-            pl.BlockSpec((hidden, hidden), lambda i: (0, 0)),
-            pl.BlockSpec((levels, hidden), lambda i: (0, 0)),
-        ],
-        out_specs=[
-            pl.BlockSpec((step, levels, width), lambda i: (i, 0, 0)),
-            pl.BlockSpec((step, rows - levels, width), lambda i: (i, 0, 0)),
-        ],
+        network_kernel,
+        in_specs=[VMEM] * 4 + [HBM] * 2,
+        out_specs=[VMEM] * 4,
         out_shape=[
             jax.ShapeDtypeStruct((senders, levels, width), BF16),
             pltpu.HBM((senders, rows - levels, width), BF16),
+            pltpu.VMEM(table.shape, BF16),
+            pltpu.VMEM(row.shape, BF16),
+        ],
+        scratch_shapes=[
+            pltpu.VMEM((levels, columns), F32),
+            pltpu.VMEM((levels, columns), F32),
+            pltpu.SemaphoreType.DMA((2,)),
         ],
         compiler_params=params(),
         cost_estimate=pl.CostEstimate(
-            flops=2 * senders * width * hidden * (hidden + 2 * 256),
+            flops=senders * width * hidden * (hidden + 2 * 256),
             bytes_accessed=4 << 20,
-            transcendentals=2 * senders * width * hidden,
+            transcendentals=senders * width * hidden,
         ),
         name="network",
-    )(arrived, first_w, middle_w, last_w)
+    )(arrived, first_w, middle_w, last_w, *in_hbm(table, row))
 
 
 def return_kernel(
-    n_lon, returned_ref, expert_hbm, cloudy_hbm, table_hbm, first_hbm, tend_ref, out_ref,
-    expert_ref, cloudy_ref, table_ref, first_ref, count_ref, rows_ref, sems
+    n_lon, returned_ref, table_ref, first_ref, expert_hbm, cloudy_hbm, tend_ref, out_ref,
+    expert_ref, cloudy_ref, used_ref, rows_ref, sems
 ):
     networks, levels, _ = returned_ref.shape
     waves = first_ref.shape[0] // 2
-    pairs = (
-        (expert_hbm, expert_ref), (cloudy_hbm, cloudy_ref), (table_hbm, table_ref), (first_hbm, first_ref),
-    )
+    pairs = ((expert_hbm, expert_ref), (cloudy_hbm, cloudy_ref))
     fetches = [
         pltpu.make_async_copy(source, target, sems.at[i]) for i, (source, target) in enumerate(pairs)
     ]
@@ -250,19 +303,23 @@
         fetch.start()
     lanes = lax.broadcasted_iota(jnp.int32, (levels, CMAX), 1)
     for network in range(networks):
-        count_ref[network] = 0
-    for fetch in fetches[:2]:
-        fetch.wait()
+        used_ref[network] = 0
+    for fetch in fetches:
+        fetch.wait()
+    spans = []
     for block in range(NB_ROW):
         network = expert_ref[block]
-        rank = count_ref[network]
-        count_ref[network] = rank + 1
-        place = pl.ds(pl.multiple_of(rank * CMAX, CMAX), CMAX)
-        values = returned_ref[network, :, place].astype(F32)
-        kept = jnp.where(lanes < cloudy_ref[block], values, 0.0)
+        start = used_ref[network]
+        count = cloudy_ref[block]
+        used_ref[network] = start + count
+        spans.append((network, start, count))
+    for block, (network, start, count) in enumerate(spans):
+        back = lax.rem(2 * CMAX - start, CMAX)
+        near = pltpu.roll(returned_ref[network, :, :CMAX].astype(F32), back, 1)
+        far = pltpu.roll(returned_ref[network, :, CMAX:].astype(F32), back, 1)
+        values = jnp.where(lanes < CMAX - start, near, far)
+        kept = jnp.where(lanes < count, values, 0.0)
         tend_ref[:, block * CMAX : (block + 1) * CMAX] = kept.astype(BF16)
-    for fetch in fetches[2:]:
-        fetch.wait()
     out = dot_nt(table_ref[...], tend_ref[...]) * (TIME_STEP / math.sqrt(n_lon))
     out = jnp.concatenate([out, jnp.zeros((out.shape[0], LANES - levels), F32)], axis=1)
     for part in range(2):
@@ -277,7 +334,7 @@
     networks, levels, _ = returned.shape
     return pl.pallas_call(
         functools.partial(return_kernel, n_lon),
-        in_specs=[VMEM] + [HBM] * 4,
+        in_specs=[VMEM] * 3 + [HBM] * 2,
         out_specs=[VMEM] * 2,
         out_shape=[
             pltpu.HBM((levels, n_lon), BF16),
@@ -286,19 +343,17 @@
         scratch_shapes=[
             pltpu.SMEM(experts.shape, jnp.int32),
             pltpu.SMEM(cloudy.shape, jnp.int32),
-            pltpu.VMEM(table.shape, BF16),
-            pltpu.VMEM(first.shape, BF16),
             pltpu.SMEM((networks,), jnp.int32),
             pltpu.VMEM((2 * rows, LANES), F32),
-            pltpu.SemaphoreType.DMA((4,)),
+            pltpu.SemaphoreType.DMA((2,)),
         ],
         compiler_params=params(),
         name="return",
-    )(returned, *in_hbm(experts, cloudy, table, first))
+    )(returned, table, first, *in_hbm(experts, cloudy))
 
 
 def solve_kernel(
-    scale, again, me_ref, got_ref, wave_hbm, own_hbm, analysis_hbm, rate_hbm, out_ref,
+    scale, again, got_ref, wave_hbm, own_hbm, analysis_hbm, rate_hbm, out_ref,
     wave_ref, own_ref, analysis_ref, rate_ref, rows_ref, turn_ref, sems
 ):
     levels = analysis_ref.shape[0]
@@ -318,7 +373,7 @@
         fetch.wait()
     table = jnp.concatenate([own_ref[sender] for sender in range(networks)], axis=0)
 
-    wave = wave_ref[me_ref[0]]
+    wave = wave_ref[lax.axis_index("dyn") * networks + lax.axis_index("phys")]
     total = (wave + lax.broadcasted_iota(jnp.int32, (levels, coeffs), 1)).astype(F32)
     rate = jnp.concatenate([rate_ref[...], jnp.zeros((1, LANES - levels), F32)], axis=1)
     rate = jnp.broadcast_to(rate, (LANES, LANES)).T[:levels]
@@ -355,11 +410,11 @@
     out_ref[...] = turn_ref[...].astype(BF16)
 
 
-def solve_twice(scale, again, me, got, waves, own, analysis, rate):
+def solve_twice(scale, again, got, waves, own, analysis, rate):
     rows = got.shape[0]
     return pl.pallas_call(
         functools.partial(solve_kernel, scale, again),
-        in_specs=[SMEM, VMEM] + [HBM] * 4,
+        in_specs=[VMEM] + [HBM] * 4,
         out_specs=VMEM,
         out_shape=jax.ShapeDtypeStruct((rows // 2, LANES), BF16),
         scratch_shapes=[
@@ -373,7 +428,7 @@
         ],
         compiler_params=params(),
         name="solve",
-    )(me, got, *in_hbm(waves, own, analysis, rate))
+    )(got, *in_hbm(waves, own, analysis, rate))
 
 
 def synthesis_kernel(scale, home_ref, table_ref, out_ref, rows_ref):
@@ -425,7 +480,7 @@
 
     share = lats // n_phys
 
-    outgoing = place_blocks(experts, state, legendre.reshape(n_phys, share * CAP, coeffs // CAP))
+    outgoing = place_blocks(experts, cloudy_count, state, legendre.reshape(n_phys, share * CAP, coeffs // CAP))
     arrived = lax.all_to_all(outgoing, "phys", split_axis=0, concat_axis=0, tiled=True)
 
     high, low = (jnp.asarray(part) for part in wave_table(waves, n_lon))
@@ -434,11 +489,10 @@
     table, first, first_w, middle_w, last_w = prepare(
         state, prev, order, high, low, w_in[0], w_mid[0], w_out[0]
     )
-    me = lax.axis_index("dyn") * n_phys + lax.axis_index("phys")
     arrived, table, first, first_w, middle_w, last_w = lax.optimization_barrier(
         (arrived, table, first, first_w, middle_w, last_w)
     )
-    computed, own = network(arrived, first_w, middle_w, last_w)
+    computed, own, table, first = network(arrived, first_w, middle_w, last_w, table, first)
     returned = lax.all_to_all(computed, "phys", split_axis=0, concat_axis=0, tiled=True)
 
     tendency, sent = return_blocks(returned, experts, cloudy_count, table, first)
@@ -448,7 +502,6 @@
     back = solve_twice(
         1.0 / (waves * (waves + 1.0)),
         (n_lon / 2.0) / math.sqrt(waves) / math.sqrt(n_lon),
-        me.reshape(1),
         got.reshape(4 * lats, LANES),
         band_waves,
         own,

time: 106 us -> 102 us (0.962)
  blocking collectives: 34.5 us -> 60 us
  waiting for transfers between devices: 22.6 us -> 6.79 us
  starting transfers between devices: 18.8 us -> 8.46 us
  Pallas kernels: 28.9 us -> 24.7 us
    all_to_all x0 -> x1, blocking collectives: none -> 27.3 us  [on_device(): lax.all_to_all(sent.reshape(waves, 4, LANES), ORDER, split_axis=0, concat...]
    all_to_all x1 -> x0, waiting for transfers between devices: 15.8 us -> none  [on_device(): lax.all_to_all(sent.reshape(waves, 4, LANES), ORDER, split_axis=0, concat...]
    all_to_all x1 -> x0, starting transfers between devices: 10.3 us -> none  [on_device(): lax.all_to_all(sent.reshape(waves, 4, LANES), ORDER, split_axis=0, concat...]
    pallas_call x4, Pallas kernels: 20.9 us -> 16.6 us  [the longest x1 9.87 us: network(): pl.pallas_call(network_kernel, in_specs=[VMEM] * 4 + [HBM] * 2, out_specs...]
    all_to_all x1, blocking collectives: 16.1 us -> 14.3 us  [on_device(): lax.all_to_all(computed, 'phys', split_axis=0, concat_axis=0, tiled=True)]
  transfers between devices with their start and end apart: 2 -> 1, of which waited for: 2 -> 1; matrix products, arithmetic and copies ran while one was open for 0% -> 0% of each run, Pallas kernels for 6% -> 6%
where the time goes in v3:
time: 102 us; the launch traced here: 101 us
  blocking collectives  60 us (59%)
  Pallas kernels  24.7 us (24%)
  starting transfers between devices  8.46 us (8%)
  waiting for transfers between devices  6.79 us (7%)
    all_to_all x1, blocking collectives, on_device(): lax.all_to_all(sent.reshape(waves, 4, LANES), ORDER, split_axis=0, concat...  27.3 us
    all_to_all x1, blocking collectives, on_device(): lax.all_to_all(back.reshape(lats, 2, LANES), ORDER, split_axis=0, concat_...  18.4 us
    all_to_all x1, blocking collectives, on_device(): lax.all_to_all(computed, 'phys', split_axis=0, concat_axis=0, tiled=True)  14.3 us
    pallas_call x1, Pallas kernels, network(): pl.pallas_call(network_kernel, in_specs=[VMEM] * 4 + [HBM] * 2, out_specs...  9.87 us
    all_to_all x1, starting transfers between devices, on_device(): lax.all_to_all(outgoing, 'phys', split_axis=0, concat_axis=0, tiled=True)  8.46 us
    all_to_all x1, waiting for transfers between devices, on_device(): lax.all_to_all(outgoing, 'phys', split_axis=0, concat_axis=0, tiled=True)  6.79 us
    pallas_call x1, Pallas kernels, prepare(): pl.pallas_call(functools.partial(prepare_kernel, n_lon), in_specs=[VMEM]...  6.54 us
    pallas_call x1, Pallas kernels, place_blocks(): pl.pallas_call(place_kernel, in_specs=[HBM] * 4, out_specs=VMEM, out_shap...  2.48 us
  transfers between devices with their start and end apart: 1, of which 1 were waited for; matrix products, arithmetic and copies ran while one was open for 0% of the time, Pallas kernels for 6%

profile of v3, /device:TPU:1, one launch (start us, length us, event | category | flops | bytes accessed | tf_op | source)
XLA Modules:
  0.0 101.0 jit_solution(15053432414138438221)
XLA Ops:
  0.6 0.0 copy-start
  0.6 2.5 %place.1 = bf16[16,88,256]{2,1,0:T(8,128)(2,1)} custom-call(s32[16]{0:T(128)} %bitcast.26, s32[16]{0:T(128)} %cloudy_hbm.3, f32[72,16,128]{2,1,0:T(8,128)} %bitcast.20, f32[16,32,128]{2,1,0:T(8,128)} %bitcast.23), custom_call_target="tpu_custom_call" | custom-call | tf_op jit(solution)/shard_map/place/pallas_call | solution.py:109
  3.1 8.5 %all-to-all-start = ((bf16[16,88,256]{2,1,0:T(8,128)(2,1)}), bf16[16,88,256]{2,1,0:T(8,128)(2,1)S(1)}, u32[]{:S(2)}, u32[]{:S(2)}) async-start(bf16[16,88,256]{2,1,0:T(8,128)(2,1)} %place.1), calls=%async_computation | async-start | bytes 1441792 | tf_op jit(solution)/shard_map/all_to_all | solution.py:484
  11.6 0.0 copy-done
  11.6 0.1 reshape.41
  11.7 0.1 copy.17
  11.7 0.1 eq.15
  11.8 0.1 fusion.order_ref
  11.9 6.5 %prepare.1 = (bf16[512,2048]{1,0:T(8,128)(2,1)}, bf16[512,128]{1,0:T(8,128)(2,1)}, bf16[1024,72]{1,0:T(8,128)(2,1)S(1)}, bf16[1024,1024]{1,0:T(8,128)(2,1)S(1)}, bf16[72,1024]{1,0:T(8,128)(2,1)S(1)}) custom-call(bf16[256,256]{1,0:T(8,128)(2,1)S(1)} %fusion.order_ref, f32[72,16,128]{2,1,0:T(8,128)} %bitcast.21, f32[72,16,128]{2,1,0:T(8,128)} %bitcast.30, ...), custom_call_target="tpu_custom_call" | custom-call | flops 2147483648 | bytes 12582912 | tf_op jit(solution)/shard_map/prepare/pallas_call | solution.py:177
  18.5 6.8 %all-to-all-done.x_ref = bf16[16,88,256]{2,1,0:T(8,128)(2,1)S(1)} async-done(((bf16[16,88,256]{2,1,0:T(8,128)(2,1)}), bf16[16,88,256]{2,1,0:T(8,128)(2,1)S(1)}, u32[]{:S(2)}, u32[]{:S(2)}) %all-to-all-start) | async-done | bytes 720928 | tf_op jit(solution)/shard_map/all_to_all | solution.py:484
  25.3 9.9 %network.1 = (bf16[16,72,256]{2,1,0:T(8,128)(2,1)S(1)}, bf16[16,16,256]{2,1,0:T(8,128)(2,1)}, bf16[512,2048]{1,0:T(8,128)(2,1)S(1)}, bf16[512,128]{1,0:T(8,128)(2,1)S(1)}) custom-call(bf16[16,88,256]{2,1,0:T(8,128)(2,1)S(1)} %all-to-all-done.x_ref, bf16[1024,72]{1,0:T(8,128)(2,1)S(1)} %get-tuple-element.25.first_ref, ...), custom_call_target="tpu_custom_call" | custom-call | flops 6442450944 | bytes 4194304 | tf_op jit(solution)/shard_map/network/pallas_call | solution.py:267
  35.2 14.3 %all_to_all.20.returned_ref = bf16[16,72,256]{2,1,0:T(8,128)(2,1)S(1)} all-to-all(bf16[16,72,256]{2,1,0:T(8,128)(2,1)S(1)} %get-tuple-element.30), channel_id=1, replica_groups=mesh['dyn'=16,'phys'=16] {'phys'}, dimensions={0} | all-to-all | bytes 1179648 | tf_op jit(solution)/shard_map/all_to_all | solution.py:496
  49.5 2.2 %return.1 = (bf16[72,2048]{1,0:T(8,128)(2,1)}, bf16[1024,128]{1,0:T(8,128)(2,1)S(1)}) custom-call(bf16[16,72,256]{2,1,0:T(8,128)(2,1)S(1)} %all_to_all.20.returned_ref, bf16[512,2048]{1,0:T(8,128)(2,1)S(1)} %get-tuple-element.31.table_ref, bf16[512,128]{1,0:T(8,128)(2,1)S(1)} %get-tuple-element.32.first_ref, s32[16]{0:T(128)} %bitcast.27, s32[16]{0:T(128)} %cloudy_hbm.3), custom_call_target="tpu_custom_call" | custom-call | tf_op jit(solution)/shard_map/return/pallas_call | solution.py:335
  51.7 27.3 %all_to_all.21 = bf16[256,4,128]{2,1,0:T(4,128)(2,1)S(1)} all-to-all(bf16[256,4,128]{2,1,0:T(4,128)(2,1)S(1)} %bitcast.19), channel_id=1, replica_groups=mesh['dyn'=16,'phys'=16] {'phys','dyn'}, dimensions={0} | all-to-all | bytes 524288 | tf_op jit(solution)/shard_map/all_to_all | solution.py:499
  79.0 2.1 %solve.1 = bf16[512,128]{1,0:T(8,128)(2,1)S(1)} custom-call(bf16[1024,128]{1,0:T(8,128)(2,1)S(1)} %bitcast.16, s32[256]{0:T(256)} %wave_hbm.1, bf16[16,16,256]{2,1,0:T(8,128)(2,1)} %get-tuple-element.34.own_hbm, f32[72,4,128]{2,1,0:T(4,128)} %bitcast.24, f32[1,72]{1,0:T(1,128)} %bitcast.28), custom_call_target="tpu_custom_call" | custom-call | tf_op jit(solution)/shard_map/solve/pallas_call | solution.py:415
  81.1 18.4 %all_to_all.22 = bf16[256,2,128]{2,1,0:T(2,128)(2,1)S(1)} all-to-all(bf16[256,2,128]{2,1,0:T(2,128)(2,1)S(1)} %bitcast.18), channel_id=1, replica_groups=mesh['dyn'=16,'phys'=16] {'phys','dyn'}, dimensions={0} | all-to-all | bytes 262144 | tf_op jit(solution)/shard_map/all_to_all | solution.py:511
  99.5 1.5 %synthesis.1 = f32[72,16,128]{2,1,0:T(8,128)} custom-call(bf16[512,128]{1,0:T(8,128)(2,1)S(1)} %bitcast.17, bf16[512,2048]{1,0:T(8,128)(2,1)S(1)} %get-tuple-element.31.table_ref), custom_call_target="tpu_custom_call" | custom-call | tf_op jit(solution)/shard_map/synthesis/pallas_call | solution.py:446
Async XLA Ops:
  0.6 11.0 %copy-start = (s32[256]{0:T(256)S(1)}, s32[256]{0:T(256)}, u32[]{:S(2)}) copy-start(s32[256]{0:T(256)} %wave_hbm.1) | copy-start | bytes 3076
  3.1 22.2 %all-to-all-start = ((bf16[16,88,256]{2,1,0:T(8,128)(2,1)}), bf16[16,88,256]{2,1,0:T(8,128)(2,1)S(1)}, u32[]{:S(2)}, u32[]{:S(2)}) async-start(bf16[16,88,256]{2,1,0:T(8,128)(2,1)} %place.1), calls=%async_computation | async-start | bytes 1441792 | tf_op jit(solution)/shard_map/all_to_all | solution.py:484

commit v4 on v3

--- a/solution.py
+++ b/solution.py
@@ -127,14 +127,16 @@
 
 def prepare_kernel(
     n_lon, order_ref, state_hbm, prev_hbm, high_hbm, low_hbm, in_hbm, mid_hbm, last_hbm,
-    table_ref, out_ref, first_ref, middle_ref, last_ref,
-    state_ref, prev_ref, high_ref, low_ref, in_ref, mid_ref, sems
+    wave_hbm, analysis_hbm, rate_hbm,
+    table_ref, out_ref, gain_ref, pull_ref, regain_ref, first_ref, middle_ref, last_ref,
+    state_ref, prev_ref, high_ref, low_ref, in_ref, mid_ref, wave_ref, analysis_ref, rate_ref, sems
 ):
     levels, blocks, _ = state_ref.shape
     waves = order_ref.shape[0]
     pairs = (
         (mid_hbm, mid_ref), (in_hbm, in_ref), (last_hbm, last_ref),
         (high_hbm, high_ref), (state_hbm, state_ref), (prev_hbm, prev_ref), (low_hbm, low_ref),
+        (wave_hbm, wave_ref), (analysis_hbm, analysis_ref), (rate_hbm, rate_ref),
     )
     fetches = [
         pltpu.make_async_copy(source, target, sems.at[i]) for i, (source, target) in enumerate(pairs)
@@ -170,17 +172,46 @@
         rows = slice(part * waves, (part + 1) * waves)
         out_ref[rows, :] = dot(order_ref[...], natural[rows, :]).astype(BF16)
 
-
-def prepare(state, prev, order, high, low, w_in, w_mid, w_out):
+    networks = lax.axis_size("phys")
+    lats = waves
+    coeffs = gain_ref.shape[1]
+    scale = 1.0 / (waves * (waves + 1.0))
+    again = (n_lon / 2.0) / math.sqrt(waves) / math.sqrt(n_lon)
+    wave = wave_ref[lax.axis_index("dyn") * networks + lax.axis_index("phys")]
+    total = (wave + lax.broadcasted_iota(jnp.int32, (levels, coeffs), 1)).astype(F32)
+    rate = jnp.concatenate([rate_ref[...], jnp.zeros((1, LANES - levels), F32)], axis=1)
+    rate = jnp.broadcast_to(rate, (LANES, LANES)).T[:levels]
+    rate = jnp.concatenate([rate, rate], axis=1)
+    inverse = 1.0 / (1.0 + TIME_STEP * (total * (total + 1.0) * scale + rate))
+    gap = jnp.zeros((LANES - levels, coeffs), F32)
+    gains, pulls = [], []
+    for part in range(2):
+        halves = [analysis_ref[:, 2 * part + half, :] for half in range(2)]
+        pulled = TIME_STEP * rate * jnp.concatenate(halves, axis=1) * inverse
+        gains += [inverse * (1.0 / math.sqrt(lats) / math.sqrt(coeffs)), gap]
+        pulls += [pulled * (1.0 / math.sqrt(coeffs)), gap]
+    gain_ref[...] = jnp.concatenate(gains, axis=0)
+    pull_ref[...] = jnp.concatenate(pulls, axis=0)
+    real = jnp.where(wave == 0, 2.0 * again, again)
+    imag = jnp.where(wave == 0, 0.0, again)
+    lane = lax.broadcasted_iota(jnp.int32, (1, 2 * LANES), 1)
+    regain_ref[...] = jnp.where(lane < LANES, real, imag)
+
+
+def prepare(state, prev, order, high, low, w_in, w_mid, w_out, waves, analysis, rate):
     rows, n_lon = high.shape
     levels, hidden = w_in.shape
+    coeffs = analysis.shape[1] * analysis.shape[2] // 2
     return pl.pallas_call(
         functools.partial(prepare_kernel, n_lon),
-        in_specs=[VMEM] + [HBM] * 7,
-        out_specs=[VMEM] * 5,
+        in_specs=[VMEM] + [HBM] * 10,
+        out_specs=[VMEM] * 8,
         out_shape=[
             pltpu.HBM((rows, n_lon), BF16),
             pltpu.HBM((rows, LANES), BF16),
+            pltpu.HBM((2 * LANES, coeffs), F32),
+            pltpu.HBM((2 * LANES, coeffs), F32),
+            pltpu.HBM((1, 2 * LANES), F32),
             jax.ShapeDtypeStruct((hidden, levels), BF16),
             jax.ShapeDtypeStruct((hidden, hidden), BF16),
             jax.ShapeDtypeStruct((levels, hidden), BF16),
@@ -192,29 +223,30 @@
             pltpu.VMEM(low.shape, BF16),
             pltpu.VMEM(w_in.shape, BF16),
             pltpu.VMEM(w_mid.shape, BF16),
-            pltpu.SemaphoreType.DMA((7,)),
+            pltpu.SMEM(waves.shape, jnp.int32),
+            pltpu.VMEM(analysis.shape, F32),
+            pltpu.VMEM(rate.shape, F32),
+            pltpu.SemaphoreType.DMA((10,)),
         ],
         compiler_params=params(),
         cost_estimate=pl.CostEstimate(
             flops=4 * rows * n_lon * rows, bytes_accessed=12 << 20, transcendentals=0
         ),
         name="prepare",
-    )(order, *in_hbm(state, prev, high, low, w_in, w_mid, w_out))
+    )(order, *in_hbm(state, prev, high, low, w_in, w_mid, w_out, waves, analysis, rate))
 
 
 def silu(half):
     return (half + half * jnp.tanh(half)).astype(BF16)
 
 
-def network_kernel(
-    x_ref, first_ref, middle_ref, last_ref, table_hbm, row_hbm, out_ref, own_ref, table_ref, row_ref,
-    packed_ref, done_ref, sems
-):
+def network_kernel(kept, x_ref, first_ref, middle_ref, last_ref, *refs):
+    out_ref, own_ref = refs[kept : kept + 2]
+    packed_ref, done_ref, sems = refs[2 * kept + 2 :]
     senders, levels, _ = out_ref.shape
     share = x_ref.shape[1] - levels
     fetches = [
-        pltpu.make_async_copy(table_hbm, table_ref, sems.at[0]),
-        pltpu.make_async_copy(row_hbm, row_ref, sems.at[1]),
+        pltpu.make_async_copy(refs[i], refs[kept + 2 + i], sems.at[i]) for i in range(kept)
     ]
     for fetch in fetches:
         fetch.start()
@@ -241,14 +273,23 @@
         packed_ref[:, places[1]] = jnp.where(lane < shift, near, far)
         packed_ref[:, places[2]] = far
 
-    def group(index, carry):
-        place = pl.ds(pl.multiple_of(index * GROUP, GROUP), GROUP)
+    def run(place):
         one = silu(dot(first_ref[...], packed_ref[:, place].astype(BF16)))
         two = silu(dot(middle_ref[...], one))
         done_ref[:, place] = dot(last_ref[...], two)
+
+    def pair(index, carry):
+        for half in range(2):
+            run(pl.ds(pl.multiple_of((2 * index + half) * GROUP, GROUP), GROUP))
         return carry
 
-    lax.fori_loop(0, (starts[-1] + (GROUP - 1)) // GROUP, group, 0)
+    groups = (starts[-1] + (GROUP - 1)) // GROUP
+    lax.fori_loop(0, groups // 2, pair, 0)
+
+    @pl.when(lax.rem(groups, 2) == 1)
+    def _():
+        run(pl.ds(pl.multiple_of((groups - 1) * GROUP, GROUP), GROUP))
+
     for sender in range(senders):
         shift = lax.rem(starts[sender], CMAX)
         back = lax.rem(CMAX - shift, CMAX)
@@ -260,24 +301,23 @@
         fetch.wait()
 
 
-def network(arrived, first_w, middle_w, last_w, table, row):
+def network(arrived, first_w, middle_w, last_w, *kept):
     senders, rows, width = arrived.shape
     levels, hidden = last_w.shape
     columns = -(-senders * width // GROUP) * GROUP + GROUP
     return pl.pallas_call(
-        network_kernel,
-        in_specs=[VMEM] * 4 + [HBM] * 2,
-        out_specs=[VMEM] * 4,
+        functools.partial(network_kernel, len(kept)),
+        in_specs=[VMEM] * 4 + [HBM] * len(kept),
+        out_specs=[VMEM] * (2 + len(kept)),
         out_shape=[
             jax.ShapeDtypeStruct((senders, levels, width), BF16),
-            pltpu.HBM((senders, rows - levels, width), BF16),
-            pltpu.VMEM(table.shape, BF16),
-            pltpu.VMEM(row.shape, BF16),
+            pltpu.VMEM((senders, rows - levels, width), BF16),
+            *[pltpu.VMEM(array.shape, array.dtype) for array in kept],
         ],
         scratch_shapes=[
             pltpu.VMEM((levels, columns), F32),
             pltpu.VMEM((levels, columns), F32),
-            pltpu.SemaphoreType.DMA((2,)),
+            pltpu.SemaphoreType.DMA((len(kept),)),
         ],
         compiler_params=params(),
         cost_estimate=pl.CostEstimate(
@@ -286,26 +326,18 @@
             transcendentals=senders * width * hidden,
         ),
         name="network",
-    )(arrived, first_w, middle_w, last_w, *in_hbm(table, row))
+    )(arrived, first_w, middle_w, last_w, *in_hbm(*kept))
 
 
 def return_kernel(
-    n_lon, returned_ref, table_ref, first_ref, expert_hbm, cloudy_hbm, tend_ref, out_ref,
-    expert_ref, cloudy_ref, used_ref, rows_ref, sems
+    n_lon, returned_ref, table_ref, first_ref, expert_ref, cloudy_ref, tend_hbm, out_ref,
+    tend_ref, used_ref, rows_ref, sems
 ):
     networks, levels, _ = returned_ref.shape
     waves = first_ref.shape[0] // 2
-    pairs = ((expert_hbm, expert_ref), (cloudy_hbm, cloudy_ref))
-    fetches = [
-        pltpu.make_async_copy(source, target, sems.at[i]) for i, (source, target) in enumerate(pairs)
-    ]
-    for fetch in fetches:
-        fetch.start()
     lanes = lax.broadcasted_iota(jnp.int32, (levels, CMAX), 1)
     for network in range(networks):
         used_ref[network] = 0
-    for fetch in fetches:
-        fetch.wait()
     spans = []
     for block in range(NB_ROW):
         network = expert_ref[block]
@@ -320,6 +352,8 @@
         values = jnp.where(lanes < CMAX - start, near, far)
         kept = jnp.where(lanes < count, values, 0.0)
         tend_ref[:, block * CMAX : (block + 1) * CMAX] = kept.astype(BF16)
+    leave = pltpu.make_async_copy(tend_ref, tend_hbm, sems.at[0])
+    leave.start()
     out = dot_nt(table_ref[...], tend_ref[...]) * (TIME_STEP / math.sqrt(n_lon))
     out = jnp.concatenate([out, jnp.zeros((out.shape[0], LANES - levels), F32)], axis=1)
     for part in range(2):
@@ -327,6 +361,7 @@
         rows_ref[pl.ds(part, waves, stride=4), :] = first_ref[rows, :].astype(F32)
         rows_ref[pl.ds(2 + part, waves, stride=4), :] = out[rows]
     out_ref[...] = rows_ref[...].astype(BF16)
+    leave.wait()
 
 
 def return_blocks(returned, experts, cloudy, table, first):
@@ -334,64 +369,32 @@
     networks, levels, _ = returned.shape
     return pl.pallas_call(
         functools.partial(return_kernel, n_lon),
-        in_specs=[VMEM] * 3 + [HBM] * 2,
-        out_specs=[VMEM] * 2,
+        in_specs=[VMEM] * 3 + [SMEM] * 2,
+        out_specs=[HBM, VMEM],
         out_shape=[
             pltpu.HBM((levels, n_lon), BF16),
             jax.ShapeDtypeStruct((2 * rows, LANES), BF16),
         ],
         scratch_shapes=[
-            pltpu.SMEM(experts.shape, jnp.int32),
-            pltpu.SMEM(cloudy.shape, jnp.int32),
+            pltpu.VMEM((levels, n_lon), BF16),
             pltpu.SMEM((networks,), jnp.int32),
             pltpu.VMEM((2 * rows, LANES), F32),
-            pltpu.SemaphoreType.DMA((2,)),
+            pltpu.SemaphoreType.DMA((1,)),
         ],
         compiler_params=params(),
         name="return",
-    )(returned, table, first, *in_hbm(experts, cloudy))
-
-
-def solve_kernel(
-    scale, again, got_ref, wave_hbm, own_hbm, analysis_hbm, rate_hbm, out_ref,
-    wave_ref, own_ref, analysis_ref, rate_ref, rows_ref, turn_ref, sems
-):
-    levels = analysis_ref.shape[0]
-    networks, share, coeffs = own_ref.shape
+    )(returned, table, first, experts, cloudy)
+
+
+def solve_kernel(got_ref, own_ref, gain_ref, pull_ref, regain_ref, out_ref, rows_ref, turn_ref):
+    networks, share, _ = own_ref.shape
     lats = networks * share
-    pairs = (
-        (wave_hbm, wave_ref), (own_hbm, own_ref), (analysis_hbm, analysis_ref), (rate_hbm, rate_ref),
-    )
-    fetches = [
-        pltpu.make_async_copy(source, target, sems.at[i]) for i, (source, target) in enumerate(pairs)
-    ]
-    for fetch in fetches:
-        fetch.start()
     rows_ref[...] = got_ref[...].astype(F32)
     parts = [rows_ref[pl.ds(part, lats, stride=4), :].astype(BF16) for part in range(4)]
-    for fetch in fetches:
-        fetch.wait()
     table = jnp.concatenate([own_ref[sender] for sender in range(networks)], axis=0)
-
-    wave = wave_ref[lax.axis_index("dyn") * networks + lax.axis_index("phys")]
-    total = (wave + lax.broadcasted_iota(jnp.int32, (levels, coeffs), 1)).astype(F32)
-    rate = jnp.concatenate([rate_ref[...], jnp.zeros((1, LANES - levels), F32)], axis=1)
-    rate = jnp.broadcast_to(rate, (LANES, LANES)).T[:levels]
-    rate = jnp.concatenate([rate, rate], axis=1)
-    inverse = 1.0 / (1.0 + TIME_STEP * (total * (total + 1.0) * scale + rate))
-    blank = jnp.zeros((LANES - levels, coeffs), F32)
-    gains, pulls = [], []
-    for part in range(2):
-        halves = [analysis_ref[:, 2 * part + half, :] for half in range(2)]
-        pulled = TIME_STEP * rate * jnp.concatenate(halves, axis=1) * inverse
-        gains += [inverse * (1.0 / lats), blank]
-        pulls += [pulled * (1.0 / math.sqrt(coeffs)), blank]
-    gain = jnp.concatenate(gains, axis=0)
-    pull = jnp.concatenate(pulls, axis=0)
-    real = jnp.where(wave == 0, 2.0 * again, again)
-    imag = jnp.where(wave == 0, 0.0, again)
-    lane = lax.broadcasted_iota(jnp.int32, (1, 2 * LANES), 1)
-    regain = jnp.where(lane < LANES, real, imag)
+    gain = gain_ref[...]
+    pull = pull_ref[...]
+    regain = regain_ref[...]
 
     def there(value):
         both = dot_tn(jnp.concatenate(split(value), axis=1), table)
@@ -410,45 +413,53 @@
     out_ref[...] = turn_ref[...].astype(BF16)
 
 
-def solve_twice(scale, again, got, waves, own, analysis, rate):
+def solve_twice(got, own, gain, pull, regain):
     rows = got.shape[0]
     return pl.pallas_call(
-        functools.partial(solve_kernel, scale, again),
-        in_specs=[VMEM] + [HBM] * 4,
+        solve_kernel,
+        in_specs=[VMEM] * 5,
         out_specs=VMEM,
         out_shape=jax.ShapeDtypeStruct((rows // 2, LANES), BF16),
-        scratch_shapes=[
-            pltpu.SMEM(waves.shape, jnp.int32),
-            pltpu.VMEM(own.shape, BF16),
-            pltpu.VMEM(analysis.shape, F32),
-            pltpu.VMEM(rate.shape, F32),
-            pltpu.VMEM((rows, LANES), F32),
-            pltpu.VMEM((rows // 2, LANES), F32),
-            pltpu.SemaphoreType.DMA((4,)),
-        ],
+        scratch_shapes=[pltpu.VMEM((rows, LANES), F32), pltpu.VMEM((rows // 2, LANES), F32)],
         compiler_params=params(),
         name="solve",
-    )(got, *in_hbm(waves, own, analysis, rate))
-
-
-def synthesis_kernel(scale, home_ref, table_ref, out_ref, rows_ref):
+    )(got, own, gain, pull, regain)
+
+
+def synthesis_kernel(scale, home_ref, table_ref, out_hbm, rows_ref, out_ref, sems):
     levels, blocks, width = out_ref.shape
     waves = home_ref.shape[0] // 2
     rows_ref[...] = home_ref[...].astype(F32)
     parts = [rows_ref[pl.ds(part, waves, stride=2), :].astype(BF16) for part in range(2)]
-    grid = dot_tn(jnp.concatenate(parts, axis=0), table_ref[...]) * scale
-    for block in range(blocks):
-        out_ref[:, block, :] = grid[:levels, block * width : (block + 1) * width]
+    spectrum = jnp.concatenate(parts, axis=0).T
+    cut = 4
+    copies = []
+    for start in range(0, blocks, cut):
+        grid = dot(spectrum, table_ref[:, start * width : (start + cut) * width]) * scale
+        for block in range(cut):
+            out_ref[:, start + block, :] = grid[:levels, block * width : (block + 1) * width]
+        place = slice(start, start + cut)
+        copies.append(
+            pltpu.make_async_copy(out_ref.at[:, place, :], out_hbm.at[:, place, :], sems.at[start // cut])
+        )
+        copies[-1].start()
+    for copy in copies:
+        copy.wait()
 
 
 def synthesis(home, table, levels, scale):
     n_lon = table.shape[1]
+    shape = (levels, NB_ROW, n_lon // NB_ROW)
     return pl.pallas_call(
         functools.partial(synthesis_kernel, scale),
         in_specs=[VMEM] * 2,
-        out_specs=VMEM,
-        out_shape=jax.ShapeDtypeStruct((levels, NB_ROW, n_lon // NB_ROW), F32),
-        scratch_shapes=[pltpu.VMEM(home.shape, F32)],
+        out_specs=HBM,
+        out_shape=pltpu.HBM(shape, F32),
+        scratch_shapes=[
+            pltpu.VMEM(home.shape, F32),
+            pltpu.VMEM(shape, F32),
+            pltpu.SemaphoreType.DMA((NB_ROW // 4,)),
+        ],
         compiler_params=params(),
         name="synthesis",
     )(home, table)
@@ -486,28 +497,32 @@
     high, low = (jnp.asarray(part) for part in wave_table(waves, n_lon))
     chunk_waves = band_waves.reshape(n_dyn, n_phys).T.reshape(waves, 1)
     order = (chunk_waves == jnp.arange(waves, dtype=jnp.int32)[None, :]).astype(BF16)
-    table, first, first_w, middle_w, last_w = prepare(
-        state, prev, order, high, low, w_in[0], w_mid[0], w_out[0]
-    )
-    arrived, table, first, first_w, middle_w, last_w = lax.optimization_barrier(
-        (arrived, table, first, first_w, middle_w, last_w)
-    )
-    computed, own, table, first = network(arrived, first_w, middle_w, last_w, table, first)
+    table, first, gain, pull, regain, first_w, middle_w, last_w = prepare(
+        state,
+        prev,
+        order,
+        high,
+        low,
+        w_in[0],
+        w_mid[0],
+        w_out[0],
+        band_waves,
+        analysis.reshape(levels, 2 * coeffs // LANES, LANES),
+        nudge_rate[None, :],
+    )
+    arrived, first_w, middle_w, last_w, *kept = lax.optimization_barrier(
+        (arrived, first_w, middle_w, last_w, table, first, gain, pull, regain)
+    )
+    computed, own, table, first, gain, pull, regain = network(
+        arrived, first_w, middle_w, last_w, *kept
+    )
     returned = lax.all_to_all(computed, "phys", split_axis=0, concat_axis=0, tiled=True)
 
     tendency, sent = return_blocks(returned, experts, cloudy_count, table, first)
     got = lax.all_to_all(
         sent.reshape(waves, 4, LANES), ORDER, split_axis=0, concat_axis=0, tiled=True
     )
-    back = solve_twice(
-        1.0 / (waves * (waves + 1.0)),
-        (n_lon / 2.0) / math.sqrt(waves) / math.sqrt(n_lon),
-        got.reshape(4 * lats, LANES),
-        band_waves,
-        own,
-        analysis.reshape(levels, 2 * coeffs // LANES, LANES),
-        nudge_rate[None, :],
-    )
+    back = solve_twice(got.reshape(4 * lats, LANES), own, gain, pull, regain)
     home = lax.all_to_all(
         back.reshape(lats, 2, LANES), ORDER, split_axis=0, concat_axis=0, tiled=True
     )

time: 102 us -> 98.4 us (0.965)
  Pallas kernels: 24.7 us -> 19 us
  blocking collectives: 60 us -> 62.4 us
    pallas_call x2, Pallas kernels: 12 us -> 6.83 us  [the longest x1 5.74 us: network(): pl.pallas_call(functools.partial(network_kernel, len(kept)), in_specs=[VM...]
    all_to_all x1, blocking collectives: 14.3 us -> 16.1 us  [on_device(): lax.all_to_all(computed, 'phys', split_axis=0, concat_axis=0, tiled=True)]
where the time goes in v4:
time: 98.4 us; the launch traced here: 97.9 us
  blocking collectives  62.4 us (63%)
  Pallas kernels  19 us (19%)
  starting transfers between devices  8.46 us (9%)
  waiting for transfers between devices  7.05 us (7%)
    all_to_all x1, blocking collectives, on_device(): lax.all_to_all(sent.reshape(waves, 4, LANES), ORDER, split_axis=0, concat...  27.9 us
    all_to_all x1, blocking collectives, on_device(): lax.all_to_all(back.reshape(lats, 2, LANES), ORDER, split_axis=0, concat_...  18.4 us
    all_to_all x1, blocking collectives, on_device(): lax.all_to_all(computed, 'phys', split_axis=0, concat_axis=0, tiled=True)  16.1 us
    all_to_all x1, starting transfers between devices, on_device(): lax.all_to_all(outgoing, 'phys', split_axis=0, concat_axis=0, tiled=True)  8.46 us
    all_to_all x1, waiting for transfers between devices, on_device(): lax.all_to_all(outgoing, 'phys', split_axis=0, concat_axis=0, tiled=True)  7.05 us
    pallas_call x1, Pallas kernels, prepare(): pl.pallas_call(functools.partial(prepare_kernel, n_lon), in_specs=[VMEM]...  6.28 us
    pallas_call x1, Pallas kernels, network(): pl.pallas_call(functools.partial(network_kernel, len(kept)), in_specs=[VM...  5.74 us
    pallas_call x1, Pallas kernels, place_blocks(): pl.pallas_call(place_kernel, in_specs=[HBM] * 4, out_specs=VMEM, out_shap...  2.45 us
  transfers between devices with their start and end apart: 1, of which 1 were waited for; matrix products, arithmetic and copies ran while one was open for 0% of the time, Pallas kernels for 6%

profile of v4, /device:TPU:1, one launch (start us, length us, event | category | flops | bytes accessed | tf_op | source)
XLA Modules:
  0.0 97.9 jit_solution(14244636310284267127)
XLA Ops:
  0.6 0.0 copy-start.2
  0.6 2.5 %place.1 = bf16[16,88,256]{2,1,0:T(8,128)(2,1)} custom-call(s32[16]{0:T(128)} %bitcast.20, s32[16]{0:T(128)} %cloudy_ref.1, f32[72,16,128]{2,1,0:T(8,128)} %bitcast.22, f32[16,32,128]{2,1,0:T(8,128)} %bitcast.27), custom_call_target="tpu_custom_call" | custom-call | tf_op jit(solution)/shard_map/place/pallas_call | solution.py:109
  3.1 8.5 %all-to-all-start = ((bf16[16,88,256]{2,1,0:T(8,128)(2,1)}), bf16[16,88,256]{2,1,0:T(8,128)(2,1)S(1)}, u32[]{:S(2)}, u32[]{:S(2)}) async-start(bf16[16,88,256]{2,1,0:T(8,128)(2,1)} %place.1), calls=%async_computation | async-start | bytes 1441792 | tf_op jit(solution)/shard_map/all_to_all | solution.py:495
  11.6 0.0 copy-done.2
  11.6 0.1 reshape.41
  11.6 0.1 copy.17
  11.7 0.1 eq.15
  11.8 0.1 fusion.order_ref
  11.9 6.3 %prepare.1 = (bf16[512,2048]{1,0:T(8,128)(2,1)}, bf16[512,128]{1,0:T(8,128)(2,1)}, f32[256,256]{1,0:T(8,128)}, f32[256,256]{1,0:T(8,128)}, f32[1,256]{1,0:T(1,12...) custom-call(bf16[256,256]{1,0:T(8,128)(2,1)S(1)} %fusion.order_ref, ...), custom_call_target="tpu_custom_call" | custom-call | flops 2147483648 | bytes 12582912 | tf_op jit(solution)/shard_map/prepare/pallas_call | solution.py:205
  18.2 7.1 %all-to-all-done.x_ref = bf16[16,88,256]{2,1,0:T(8,128)(2,1)S(1)} async-done(((bf16[16,88,256]{2,1,0:T(8,128)(2,1)}), bf16[16,88,256]{2,1,0:T(8,128)(2,1)S(1)}, u32[]{:S(2)}, u32[]{:S(2)}) %all-to-all-start) | async-done | bytes 720928 | tf_op jit(solution)/shard_map/all_to_all | solution.py:495
  25.3 0.0 copy-start
  25.3 0.0 copy-start.1
  25.3 5.7 %network.1 = (bf16[16,72,256]{2,1,0:T(8,128)(2,1)S(1)}, bf16[16,16,256]{2,1,0:T(8,128)(2,1)S(1)}, bf16[512,2048]{1,0:T(8,128)(2,1)S(1)}, bf16[512,128]{1,0:T(8,1...) custom-call(bf16[16,88,256]{2,1,0:T(8,128)(2,1)S(1)} %all-to-all-done.x_ref, ...), custom_call_target="tpu_custom_call" | custom-call | flops 6442450944 | bytes 4194304 | tf_op jit(solution)/shard_map/network/pallas_call | solution.py:308
  31.0 16.1 %all_to_all.20.returned_ref = bf16[16,72,256]{2,1,0:T(8,128)(2,1)S(1)} all-to-all(bf16[16,72,256]{2,1,0:T(8,128)(2,1)S(1)} %get-tuple-element.45), channel_id=1, replica_groups=mesh['dyn'=16,'phys'=16] {'phys'}, dimensions={0} | all-to-all | bytes 1179648 | tf_op jit(solution)/shard_map/all_to_all | solution.py:519
  47.1 0.0 copy-done
  47.1 0.0 copy-done.1
  47.1 2.1 %return.1 = (bf16[72,2048]{1,0:T(8,128)(2,1)}, bf16[1024,128]{1,0:T(8,128)(2,1)S(1)}) custom-call(bf16[16,72,256]{2,1,0:T(8,128)(2,1)S(1)} %all_to_all.20.returned_ref, bf16[512,2048]{1,0:T(8,128)(2,1)S(1)} %get-tuple-element.46.table_ref, bf16[512,128]{1,0:T(8,128)(2,1)S(1)} %get-tuple-element.47.first_ref, s32[16]{0:T(128)S(1)} %bitcast.21, s32[16]{0:T(128)S(1)} %copy-done.1), custom_call_target="tpu_custom_call" | custom-call | tf_op jit(solution)/shard_map/return/pallas_call | solution.py:370
  49.2 27.9 %all_to_all.21 = bf16[256,4,128]{2,1,0:T(4,128)(2,1)S(1)} all-to-all(bf16[256,4,128]{2,1,0:T(4,128)(2,1)S(1)} %bitcast.19), channel_id=1, replica_groups=mesh['dyn'=16,'phys'=16] {'phys','dyn'}, dimensions={0} | all-to-all | bytes 524288 | tf_op jit(solution)/shard_map/all_to_all | solution.py:522
  77.0 1.1 %solve.1 = bf16[512,128]{1,0:T(8,128)(2,1)S(1)} custom-call(bf16[1024,128]{1,0:T(8,128)(2,1)S(1)} %bitcast.16, bf16[16,16,256]{2,1,0:T(8,128)(2,1)S(1)} %get-tuple-element.49.own_ref, f32[256,256]{1,0:T(8,128)S(1)} %get-tuple-element.50.gain_ref, f32[256,256]{1,0:T(8,128)S(1)} %get-tuple-element.51.pull_ref, f32[1,256]{1,0:T(1,128)S(1)} %get-tuple-element.52.regain_ref), custom_call_target="tpu_custom_call" | custom-call | tf_op jit(solution)/shard_map/solve/pallas_call | solution.py:418
  78.1 18.4 %all_to_all.22 = bf16[256,2,128]{2,1,0:T(2,128)(2,1)S(1)} all-to-all(bf16[256,2,128]{2,1,0:T(2,128)(2,1)S(1)} %bitcast.17), channel_id=1, replica_groups=mesh['dyn'=16,'phys'=16] {'phys','dyn'}, dimensions={0} | all-to-all | bytes 262144 | tf_op jit(solution)/shard_map/all_to_all | solution.py:526
  96.5 1.4 %synthesis.1 = f32[72,16,128]{2,1,0:T(8,128)} custom-call(bf16[512,128]{1,0:T(8,128)(2,1)S(1)} %bitcast.18, bf16[512,2048]{1,0:T(8,128)(2,1)S(1)} %get-tuple-element.46.table_ref), custom_call_target="tpu_custom_call" | custom-call | tf_op jit(solution)/shard_map/synthesis/pallas_call | solution.py:453
Async XLA Ops:
  0.6 10.9 %copy-start.2 = (s32[256]{0:T(256)S(1)}, s32[256]{0:T(256)}, u32[]{:S(2)}) copy-start(s32[256]{0:T(256)} %wave_hbm.1) | copy-start | bytes 3076
  3.1 22.2 %all-to-all-start = ((bf16[16,88,256]{2,1,0:T(8,128)(2,1)}), bf16[16,88,256]{2,1,0:T(8,128)(2,1)S(1)}, u32[]{:S(2)}, u32[]{:S(2)}) async-start(bf16[16,88,256]{2,1,0:T(8,128)(2,1)} %place.1), calls=%async_computation | async-start | bytes 1441792 | tf_op jit(solution)/shard_map/all_to_all | solution.py:495
  25.3 21.9 %copy-start = (s32[16,1]{0,1:T(1,128)S(1)}, s32[16,1]{0,1:T(1,128)}, u32[]{:S(2)}) copy-start(s32[16,1]{0,1:T(1,128)} %param.20) | copy-start | bytes 196
  25.3 21.9 %copy-start.1 = (s32[16]{0:T(128)S(1)}, s32[16]{0:T(128)}, u32[]{:S(2)}) copy-start(s32[16]{0:T(128)} %cloudy_ref.1) | copy-start | bytes 196

commit v5 on v4

--- a/solution.py
+++ b/solution.py
@@ -273,22 +273,32 @@
         packed_ref[:, places[1]] = jnp.where(lane < shift, near, far)
         packed_ref[:, places[2]] = far
 
-    def run(place):
-        one = silu(dot(first_ref[...], packed_ref[:, place].astype(BF16)))
-        two = silu(dot(middle_ref[...], one))
+    def run(start, width, step):
+        place = pl.ds(pl.multiple_of(start, width), width)
+        columns = packed_ref[:, place].astype(BF16)
+        cuts = [slice(row, row + step) for row in range(0, middle_ref.shape[0], step)]
+        one = jnp.concatenate([silu(dot(first_ref[cut, :], columns)) for cut in cuts], axis=0)
+        two = jnp.concatenate([silu(dot(middle_ref[cut, :], one)) for cut in cuts], axis=0)
         done_ref[:, place] = dot(last_ref[...], two)
 
-    def pair(index, carry):
-        for half in range(2):
-            run(pl.ds(pl.multiple_of((2 * index + half) * GROUP, GROUP), GROUP))
+    def four(index, carry):
+        for i in range(4):
+            run((4 * index + i) * GROUP, GROUP, middle_ref.shape[0])
         return carry
 
-    groups = (starts[-1] + (GROUP - 1)) // GROUP
-    lax.fori_loop(0, groups // 2, pair, 0)
-
-    @pl.when(lax.rem(groups, 2) == 1)
+    def single(index, carry):
+        run(index * GROUP, GROUP, middle_ref.shape[0])
+        return carry
+
+    half = GROUP // 2
+    halves = (starts[-1] + (half - 1)) // half
+    groups = halves // 2
+    lax.fori_loop(0, groups // 4, four, 0)
+    lax.fori_loop(groups // 4 * 4, groups, single, 0)
+
+    @pl.when(lax.rem(halves, 2) == 1)
     def _():
-        run(pl.ds(pl.multiple_of((groups - 1) * GROUP, GROUP), GROUP))
+        run((halves - 1) * half, half, half)
 
     for sender in range(senders):
         shift = lax.rem(starts[sender], CMAX)

time: 98.4 us -> 98.4 us (level)
  Pallas kernels: 19 us -> 17.5 us
  blocking collectives: 62.4 us -> 63.7 us
    all_to_all x1, blocking collectives: 16.1 us -> 18.9 us  [on_device(): lax.all_to_all(computed, 'phys', split_axis=0, concat_axis=0, tiled=True)]
    pallas_call x1, Pallas kernels: 5.74 us -> 4.21 us  [network(): pl.pallas_call(functools.partial(network_kernel, len(kept)), in_specs=[VM...]
    all_to_all x1, blocking collectives: 27.9 us -> 26.5 us  [on_device(): lax.all_to_all(sent.reshape(waves, 4, LANES), ORDER, split_axis=0, concat...]
where the time goes in v5:
time: 98.4 us; the launch traced here: 97.9 us
  blocking collectives  63.7 us (65%)
  Pallas kernels  17.5 us (18%)
  starting transfers between devices  8.46 us (9%)
  waiting for transfers between devices  7.05 us (7%)
    all_to_all x1, blocking collectives, on_device(): lax.all_to_all(sent.reshape(waves, 4, LANES), ORDER, split_axis=0, concat...  26.5 us
    all_to_all x1, blocking collectives, on_device(): lax.all_to_all(computed, 'phys', split_axis=0, concat_axis=0, tiled=True)  18.9 us
    all_to_all x1, blocking collectives, on_device(): lax.all_to_all(back.reshape(lats, 2, LANES), ORDER, split_axis=0, concat_...  18.4 us
    all_to_all x1, starting transfers between devices, on_device(): lax.all_to_all(outgoing, 'phys', split_axis=0, concat_axis=0, tiled=True)  8.46 us
    all_to_all x1, waiting for transfers between devices, on_device(): lax.all_to_all(outgoing, 'phys', split_axis=0, concat_axis=0, tiled=True)  7.05 us
    pallas_call x1, Pallas kernels, prepare(): pl.pallas_call(functools.partial(prepare_kernel, n_lon), in_specs=[VMEM]...  6.28 us
    pallas_call x1, Pallas kernels, network(): pl.pallas_call(functools.partial(network_kernel, len(kept)), in_specs=[VM...  4.21 us
    pallas_call x1, Pallas kernels, place_blocks(): pl.pallas_call(place_kernel, in_specs=[HBM] * 4, out_specs=VMEM, out_shap...  2.45 us
  transfers between devices with their start and end apart: 1, of which 1 were waited for; matrix products, arithmetic and copies ran while one was open for 0% of the time, Pallas kernels for 6%

profile of v5, /device:TPU:1, one launch (start us, length us, event | category | flops | bytes accessed | tf_op | source)
XLA Modules:
  0.0 97.9 jit_solution(9542148899783121778)
XLA Ops:
  0.6 0.0 copy-start.2
  0.6 2.5 %place.1 = bf16[16,88,256]{2,1,0:T(8,128)(2,1)} custom-call(s32[16]{0:T(128)} %bitcast.20, s32[16]{0:T(128)} %cloudy_ref.1, f32[72,16,128]{2,1,0:T(8,128)} %bitcast.22, f32[16,32,128]{2,1,0:T(8,128)} %bitcast.27), custom_call_target="tpu_custom_call" | custom-call | tf_op jit(solution)/shard_map/place/pallas_call | solution.py:109
  3.1 8.5 %all-to-all-start = ((bf16[16,88,256]{2,1,0:T(8,128)(2,1)}), bf16[16,88,256]{2,1,0:T(8,128)(2,1)S(1)}, u32[]{:S(2)}, u32[]{:S(2)}) async-start(bf16[16,88,256]{2,1,0:T(8,128)(2,1)} %place.1), calls=%async_computation | async-start | bytes 1441792 | tf_op jit(solution)/shard_map/all_to_all | solution.py:505
  11.6 0.0 copy-done.2
  11.6 0.1 reshape.41
  11.6 0.1 copy.17
  11.7 0.1 eq.15
  11.8 0.1 fusion.order_ref
  11.9 6.3 %prepare.1 = (bf16[512,2048]{1,0:T(8,128)(2,1)}, bf16[512,128]{1,0:T(8,128)(2,1)}, f32[256,256]{1,0:T(8,128)}, f32[256,256]{1,0:T(8,128)}, f32[1,256]{1,0:T(1,12...) custom-call(bf16[256,256]{1,0:T(8,128)(2,1)S(1)} %fusion.order_ref, ...), custom_call_target="tpu_custom_call" | custom-call | flops 2147483648 | bytes 12582912 | tf_op jit(solution)/shard_map/prepare/pallas_call | solution.py:205
  18.2 7.0 %all-to-all-done.x_ref = bf16[16,88,256]{2,1,0:T(8,128)(2,1)S(1)} async-done(((bf16[16,88,256]{2,1,0:T(8,128)(2,1)}), bf16[16,88,256]{2,1,0:T(8,128)(2,1)S(1)}, u32[]{:S(2)}, u32[]{:S(2)}) %all-to-all-start) | async-done | bytes 720928 | tf_op jit(solution)/shard_map/all_to_all | solution.py:505
  25.3 0.0 copy-start
  25.3 0.0 copy-start.1
  25.3 4.2 %network.1 = (bf16[16,72,256]{2,1,0:T(8,128)(2,1)S(1)}, bf16[16,16,256]{2,1,0:T(8,128)(2,1)S(1)}, bf16[512,2048]{1,0:T(8,128)(2,1)S(1)}, bf16[512,128]{1,0:T(8,1...) custom-call(bf16[16,88,256]{2,1,0:T(8,128)(2,1)S(1)} %all-to-all-done.x_ref, ...), custom_call_target="tpu_custom_call" | custom-call | flops 6442450944 | bytes 4194304 | tf_op jit(solution)/shard_map/network/pallas_call | solution.py:318
  29.5 18.9 %all_to_all.20.returned_ref = bf16[16,72,256]{2,1,0:T(8,128)(2,1)S(1)} all-to-all(bf16[16,72,256]{2,1,0:T(8,128)(2,1)S(1)} %get-tuple-element.45), channel_id=1, replica_groups=mesh['dyn'=16,'phys'=16] {'phys'}, dimensions={0} | all-to-all | bytes 1179648 | tf_op jit(solution)/shard_map/all_to_all | solution.py:529
  48.3 0.0 copy-done
  48.3 0.0 copy-done.1
  48.3 2.1 %return.1 = (bf16[72,2048]{1,0:T(8,128)(2,1)}, bf16[1024,128]{1,0:T(8,128)(2,1)S(1)}) custom-call(bf16[16,72,256]{2,1,0:T(8,128)(2,1)S(1)} %all_to_all.20.returned_ref, bf16[512,2048]{1,0:T(8,128)(2,1)S(1)} %get-tuple-element.46.table_ref, bf16[512,128]{1,0:T(8,128)(2,1)S(1)} %get-tuple-element.47.first_ref, s32[16]{0:T(128)S(1)} %bitcast.21, s32[16]{0:T(128)S(1)} %copy-done.1), custom_call_target="tpu_custom_call" | custom-call | tf_op jit(solution)/shard_map/return/pallas_call | solution.py:380
  50.4 26.5 %all_to_all.21 = bf16[256,4,128]{2,1,0:T(4,128)(2,1)S(1)} all-to-all(bf16[256,4,128]{2,1,0:T(4,128)(2,1)S(1)} %bitcast.19), channel_id=1, replica_groups=mesh['dyn'=16,'phys'=16] {'phys','dyn'}, dimensions={0} | all-to-all | bytes 524288 | tf_op jit(solution)/shard_map/all_to_all | solution.py:532
  76.9 1.1 %solve.1 = bf16[512,128]{1,0:T(8,128)(2,1)S(1)} custom-call(bf16[1024,128]{1,0:T(8,128)(2,1)S(1)} %bitcast.16, bf16[16,16,256]{2,1,0:T(8,128)(2,1)S(1)} %get-tuple-element.49.own_ref, f32[256,256]{1,0:T(8,128)S(1)} %get-tuple-element.50.gain_ref, f32[256,256]{1,0:T(8,128)S(1)} %get-tuple-element.51.pull_ref, f32[1,256]{1,0:T(1,128)S(1)} %get-tuple-element.52.regain_ref), custom_call_target="tpu_custom_call" | custom-call | tf_op jit(solution)/shard_map/solve/pallas_call | solution.py:428
  77.9 18.4 %all_to_all.22 = bf16[256,2,128]{2,1,0:T(2,128)(2,1)S(1)} all-to-all(bf16[256,2,128]{2,1,0:T(2,128)(2,1)S(1)} %bitcast.17), channel_id=1, replica_groups=mesh['dyn'=16,'phys'=16] {'phys','dyn'}, dimensions={0} | all-to-all | bytes 262144 | tf_op jit(solution)/shard_map/all_to_all | solution.py:536
  96.3 1.4 %synthesis.1 = f32[72,16,128]{2,1,0:T(8,128)} custom-call(bf16[512,128]{1,0:T(8,128)(2,1)S(1)} %bitcast.18, bf16[512,2048]{1,0:T(8,128)(2,1)S(1)} %get-tuple-element.46.table_ref), custom_call_target="tpu_custom_call" | custom-call | tf_op jit(solution)/shard_map/synthesis/pallas_call | solution.py:463
Async XLA Ops:
  0.6 10.9 %copy-start.2 = (s32[256]{0:T(256)S(1)}, s32[256]{0:T(256)}, u32[]{:S(2)}) copy-start(s32[256]{0:T(256)} %wave_hbm.1) | copy-start | bytes 3076
  3.1 22.2 %all-to-all-start = ((bf16[16,88,256]{2,1,0:T(8,128)(2,1)}), bf16[16,88,256]{2,1,0:T(8,128)(2,1)S(1)}, u32[]{:S(2)}, u32[]{:S(2)}) async-start(bf16[16,88,256]{2,1,0:T(8,128)(2,1)} %place.1), calls=%async_computation | async-start | bytes 1441792 | tf_op jit(solution)/shard_map/all_to_all | solution.py:505
  25.3 23.1 %copy-start = (s32[16,1]{0,1:T(1,128)S(1)}, s32[16,1]{0,1:T(1,128)}, u32[]{:S(2)}) copy-start(s32[16,1]{0,1:T(1,128)} %param.20) | copy-start | bytes 196
  25.3 23.1 %copy-start.1 = (s32[16]{0:T(128)S(1)}, s32[16]{0:T(128)}, u32[]{:S(2)}) copy-start(s32[16]{0:T(128)} %cloudy_ref.1) | copy-start | bytes 196

commit v6 on v5

--- a/solution.py
+++ b/solution.py
@@ -59,17 +59,16 @@
 
 
 def place_kernel(
-    expert_hbm, cloudy_hbm, state_hbm, legendre_hbm, out_ref,
-    expert_ref, cloudy_ref, state_ref, legendre_ref, chunk_ref, used_ref, sems
+    expert_hbm, cloudy_hbm, state_hbm, out_ref,
+    expert_ref, cloudy_ref, state_ref, chunk_ref, used_ref, sems
 ):
     networks, _, width = out_ref.shape
     blocks, levels, _ = state_ref.shape
-    share = legendre_ref.shape[1] // CAP
     fetches = [
         pltpu.make_async_copy(state_hbm.at[:, block, :], state_ref.at[block], sems.at[block])
         for block in range(blocks)
     ]
-    pairs = ((expert_hbm, expert_ref), (cloudy_hbm, cloudy_ref), (legendre_hbm, legendre_ref))
+    pairs = ((expert_hbm, expert_ref), (cloudy_hbm, cloudy_ref))
     early = [
         pltpu.make_async_copy(source, target, sems.at[blocks + i])
         for i, (source, target) in enumerate(pairs)
@@ -81,10 +80,6 @@
         used_ref[network] = 0
     for fetch in early:
         fetch.wait()
-    for network in range(networks):
-        for half in range(CAP):
-            part = legendre_ref[network, pl.ds(half, share, stride=CAP), :]
-            out_ref[network, :share, half * CMAX : (half + 1) * CMAX] = part.astype(BF16)
     lane = lax.broadcasted_iota(jnp.int32, (levels, CMAX), 1)
     spans = []
     for block in range(blocks):
@@ -100,36 +95,35 @@
         here = (lane >= start) & (lane < end)
         pltpu.store(chunk_ref.at[network, :, :CMAX], turned, mask=here)
         pltpu.store(chunk_ref.at[network, :, CMAX:], turned, mask=lane + CMAX < end)
-    out_ref[:, share:, :] = chunk_ref[...].astype(BF16)
-
-
-def place_blocks(experts, cloudy, state, legendre):
+    out_ref[...] = chunk_ref[...].astype(BF16)
+
+
+def place_blocks(experts, cloudy, state, networks):
     levels, blocks, width = state.shape
-    networks, share, _ = legendre.shape
     return pl.pallas_call(
         place_kernel,
-        in_specs=[HBM] * 4,
+        in_specs=[HBM] * 3,
         out_specs=VMEM,
-        out_shape=pltpu.HBM((networks, share // CAP + levels, CAP * CMAX), BF16),
+        out_shape=pltpu.HBM((networks, levels, CAP * CMAX), BF16),
         scratch_shapes=[
             pltpu.SMEM((blocks,), jnp.int32),
             pltpu.SMEM((blocks,), jnp.int32),
             pltpu.VMEM((blocks, levels, width), F32),
-            pltpu.VMEM(legendre.shape, F32),
             pltpu.VMEM((networks, levels, CAP * CMAX), F32),
             pltpu.SMEM((networks,), jnp.int32),
-            pltpu.SemaphoreType.DMA((blocks + 3,)),
+            pltpu.SemaphoreType.DMA((blocks + 2,)),
         ],
         compiler_params=params(),
         name="place",
-    )(*in_hbm(experts, cloudy, state, legendre))
+    )(*in_hbm(experts, cloudy, state))
 
 
 def prepare_kernel(
     n_lon, order_ref, state_hbm, prev_hbm, high_hbm, low_hbm, in_hbm, mid_hbm, last_hbm,
-    wave_hbm, analysis_hbm, rate_hbm,
-    table_ref, out_ref, gain_ref, pull_ref, regain_ref, first_ref, middle_ref, last_ref,
-    state_ref, prev_ref, high_ref, low_ref, in_ref, mid_ref, wave_ref, analysis_ref, rate_ref, sems
+    wave_hbm, analysis_hbm, rate_hbm, legendre_hbm,
+    table_ref, out_ref, gain_ref, pull_ref, regain_ref, share_ref, first_ref, middle_ref, last_ref,
+    state_ref, prev_ref, high_ref, low_ref, in_ref, mid_ref, wave_ref, analysis_ref, rate_ref, legendre_ref,
+    sems
 ):
     levels, blocks, _ = state_ref.shape
     waves = order_ref.shape[0]
@@ -137,6 +131,7 @@
         (mid_hbm, mid_ref), (in_hbm, in_ref), (last_hbm, last_ref),
         (high_hbm, high_ref), (state_hbm, state_ref), (prev_hbm, prev_ref), (low_hbm, low_ref),
         (wave_hbm, wave_ref), (analysis_hbm, analysis_ref), (rate_hbm, rate_ref),
+        (legendre_hbm, legendre_ref),
     )
     fetches = [
         pltpu.make_async_copy(source, target, sems.at[i]) for i, (source, target) in enumerate(pairs)
@@ -172,7 +167,11 @@
         rows = slice(part * waves, (part + 1) * waves)
         out_ref[rows, :] = dot(order_ref[...], natural[rows, :]).astype(BF16)
 
-    networks = lax.axis_size("phys")
+    networks, share, _ = share_ref.shape
+    for network in range(networks):
+        for half in range(CAP):
+            part = legendre_ref[network, pl.ds(half, share, stride=CAP), :]
+            share_ref[network, :, half * CMAX : (half + 1) * CMAX] = part.astype(BF16)
     lats = waves
     coeffs = gain_ref.shape[1]
     scale = 1.0 / (waves * (waves + 1.0))
@@ -198,20 +197,21 @@
     regain_ref[...] = jnp.where(lane < LANES, real, imag)
 
 
-def prepare(state, prev, order, high, low, w_in, w_mid, w_out, waves, analysis, rate):
+def prepare(state, prev, order, high, low, w_in, w_mid, w_out, waves, analysis, rate, legendre):
     rows, n_lon = high.shape
     levels, hidden = w_in.shape
     coeffs = analysis.shape[1] * analysis.shape[2] // 2
     return pl.pallas_call(
         functools.partial(prepare_kernel, n_lon),
-        in_specs=[VMEM] + [HBM] * 10,
-        out_specs=[VMEM] * 8,
+        in_specs=[VMEM] + [HBM] * 11,
+        out_specs=[VMEM] * 9,
         out_shape=[
             pltpu.HBM((rows, n_lon), BF16),
             pltpu.HBM((rows, LANES), BF16),
             pltpu.HBM((2 * LANES, coeffs), F32),
             pltpu.HBM((2 * LANES, coeffs), F32),
             pltpu.HBM((1, 2 * LANES), F32),
+            pltpu.HBM((legendre.shape[0], legendre.shape[1] // CAP, coeffs), BF16),
             jax.ShapeDtypeStruct((hidden, levels), BF16),
             jax.ShapeDtypeStruct((hidden, hidden), BF16),
             jax.ShapeDtypeStruct((levels, hidden), BF16),
@@ -226,14 +226,15 @@
             pltpu.SMEM(waves.shape, jnp.int32),
             pltpu.VMEM(analysis.shape, F32),
             pltpu.VMEM(rate.shape, F32),
-            pltpu.SemaphoreType.DMA((10,)),
+            pltpu.VMEM(legendre.shape, F32),
+            pltpu.SemaphoreType.DMA((11,)),
         ],
         compiler_params=params(),
         cost_estimate=pl.CostEstimate(
             flops=4 * rows * n_lon * rows, bytes_accessed=12 << 20, transcendentals=0
         ),
         name="prepare",
-    )(order, *in_hbm(state, prev, high, low, w_in, w_mid, w_out, waves, analysis, rate))
+    )(order, *in_hbm(state, prev, high, low, w_in, w_mid, w_out, waves, analysis, rate, legendre))
 
 
 def silu(half):
@@ -241,17 +242,16 @@
 
 
 def network_kernel(kept, x_ref, first_ref, middle_ref, last_ref, *refs):
-    out_ref, own_ref = refs[kept : kept + 2]
+    share_hbm, out_ref = refs[kept : kept + 2]
     packed_ref, done_ref, sems = refs[2 * kept + 2 :]
-    senders, levels, _ = out_ref.shape
-    share = x_ref.shape[1] - levels
+    senders, levels, _ = x_ref.shape
+    share = share_hbm.shape[1]
     fetches = [
         pltpu.make_async_copy(refs[i], refs[kept + 2 + i], sems.at[i]) for i in range(kept)
-    ]
+    ] + [pltpu.make_async_copy(share_hbm, out_ref.at[:, :share, :], sems.at[kept])]
     for fetch in fetches:
         fetch.start()
-    own_ref[...] = x_ref[:, :share, :]
-    heads = [x_ref[sender, share : share + 16, :].astype(F32)[:1] for sender in range(senders)]
+    heads = [x_ref[sender, :16, :].astype(F32)[:1] for sender in range(senders)]
     marked = jnp.where(jnp.concatenate(heads, axis=0) < 0.1 * MARK, 1.0, 0.0)
     marked = marked[:, :CMAX] + marked[:, CMAX:]
     lane = lax.broadcasted_iota(jnp.int32, (levels, CMAX), 1)
@@ -267,8 +267,8 @@
     for sender in range(senders):
         shift = lax.rem(starts[sender], CMAX)
         places = tiles(starts[sender])
-        near = pltpu.roll(x_ref[sender, share:, :CMAX].astype(F32), shift, 1)
-        far = pltpu.roll(x_ref[sender, share:, CMAX:].astype(F32), shift, 1)
+        near = pltpu.roll(x_ref[sender, :, :CMAX].astype(F32), shift, 1)
+        far = pltpu.roll(x_ref[sender, :, CMAX:].astype(F32), shift, 1)
         packed_ref[:, places[0]] = jnp.where(lane < shift, packed_ref[:, places[0]], near)
         packed_ref[:, places[1]] = jnp.where(lane < shift, near, far)
         packed_ref[:, places[2]] = far
@@ -283,7 +283,7 @@
 
     def four(index, carry):
         for i in range(4):
-            run((4 * index + i) * GROUP, GROUP, middle_ref.shape[0])
+            run((4 * index + i) * GROUP, GROUP, 256)
         return carry
 
     def single(index, carry):
@@ -305,29 +305,29 @@
         back = lax.rem(CMAX - shift, CMAX)
         near, middle, far = (pltpu.roll(done_ref[:, place], back, 1) for place in tiles(starts[sender]))
         keep = lane < CMAX - shift
-        out_ref[sender, :, :CMAX] = jnp.where(keep, near, middle).astype(BF16)
-        out_ref[sender, :, CMAX:] = jnp.where(keep, middle, far).astype(BF16)
+        out_ref[sender, share:, :CMAX] = jnp.where(keep, near, middle).astype(BF16)
+        out_ref[sender, share:, CMAX:] = jnp.where(keep, middle, far).astype(BF16)
     for fetch in fetches:
         fetch.wait()
 
 
-def network(arrived, first_w, middle_w, last_w, *kept):
-    senders, rows, width = arrived.shape
-    levels, hidden = last_w.shape
+def network(arrived, first_w, middle_w, last_w, shares, *kept):
+    senders, levels, width = arrived.shape
+    share = shares.shape[1]
+    hidden = last_w.shape[1]
     columns = -(-senders * width // GROUP) * GROUP + GROUP
     return pl.pallas_call(
         functools.partial(network_kernel, len(kept)),
-        in_specs=[VMEM] * 4 + [HBM] * len(kept),
-        out_specs=[VMEM] * (2 + len(kept)),
+        in_specs=[VMEM] * 4 + [HBM] * (1 + len(kept)),
+        out_specs=[VMEM] * (1 + len(kept)),
         out_shape=[
-            jax.ShapeDtypeStruct((senders, levels, width), BF16),
-            pltpu.VMEM((senders, rows - levels, width), BF16),
+            jax.ShapeDtypeStruct((senders, share + levels, width), BF16),
             *[pltpu.VMEM(array.shape, array.dtype) for array in kept],
         ],
         scratch_shapes=[
             pltpu.VMEM((levels, columns), F32),
             pltpu.VMEM((levels, columns), F32),
-            pltpu.SemaphoreType.DMA((len(kept),)),
+            pltpu.SemaphoreType.DMA((1 + len(kept),)),
         ],
         compiler_params=params(),
         cost_estimate=pl.CostEstimate(
@@ -336,14 +336,16 @@
             transcendentals=senders * width * hidden,
         ),
         name="network",
-    )(arrived, first_w, middle_w, last_w, *in_hbm(*kept))
+    )(arrived, first_w, middle_w, last_w, *in_hbm(*kept, shares))
 
 
 def return_kernel(
     n_lon, returned_ref, table_ref, first_ref, expert_ref, cloudy_ref, tend_hbm, out_ref,
     tend_ref, used_ref, rows_ref, sems
 ):
-    networks, levels, _ = returned_ref.shape
+    networks = returned_ref.shape[0]
+    levels = tend_ref.shape[0]
+    share = returned_ref.shape[1] - levels
     waves = first_ref.shape[0] // 2
     lanes = lax.broadcasted_iota(jnp.int32, (levels, CMAX), 1)
     for network in range(networks):
@@ -357,8 +359,8 @@
         spans.append((network, start, count))
     for block, (network, start, count) in enumerate(spans):
         back = lax.rem(2 * CMAX - start, CMAX)
-        near = pltpu.roll(returned_ref[network, :, :CMAX].astype(F32), back, 1)
-        far = pltpu.roll(returned_ref[network, :, CMAX:].astype(F32), back, 1)
+        near = pltpu.roll(returned_ref[network, share:, :CMAX].astype(F32), back, 1)
+        far = pltpu.roll(returned_ref[network, share:, CMAX:].astype(F32), back, 1)
         values = jnp.where(lanes < CMAX - start, near, far)
         kept = jnp.where(lanes < count, values, 0.0)
         tend_ref[:, block * CMAX : (block + 1) * CMAX] = kept.astype(BF16)
@@ -374,9 +376,9 @@
     leave.wait()
 
 
-def return_blocks(returned, experts, cloudy, table, first):
+def return_blocks(levels, returned, experts, cloudy, table, first):
     rows, n_lon = table.shape
-    networks, levels, _ = returned.shape
+    networks = returned.shape[0]
     return pl.pallas_call(
         functools.partial(return_kernel, n_lon),
         in_specs=[VMEM] * 3 + [SMEM] * 2,
@@ -396,12 +398,12 @@
     )(returned, table, first, experts, cloudy)
 
 
-def solve_kernel(got_ref, own_ref, gain_ref, pull_ref, regain_ref, out_ref, rows_ref, turn_ref):
-    networks, share, _ = own_ref.shape
+def solve_kernel(share, got_ref, own_ref, gain_ref, pull_ref, regain_ref, out_ref, rows_ref, turn_ref):
+    networks = own_ref.shape[0]
     lats = networks * share
     rows_ref[...] = got_ref[...].astype(F32)
     parts = [rows_ref[pl.ds(part, lats, stride=4), :].astype(BF16) for part in range(4)]
-    table = jnp.concatenate([own_ref[sender] for sender in range(networks)], axis=0)
+    table = jnp.concatenate([own_ref[sender, :share, :] for sender in range(networks)], axis=0)
     gain = gain_ref[...]
     pull = pull_ref[...]
     regain = regain_ref[...]
@@ -423,10 +425,10 @@
     out_ref[...] = turn_ref[...].astype(BF16)
 
 
-def solve_twice(got, own, gain, pull, regain):
+def solve_twice(share, got, own, gain, pull, regain):
     rows = got.shape[0]
     return pl.pallas_call(
-        solve_kernel,
+        functools.partial(solve_kernel, share),
         in_specs=[VMEM] * 5,
         out_specs=VMEM,
         out_shape=jax.ShapeDtypeStruct((rows // 2, LANES), BF16),
@@ -501,13 +503,13 @@
 
     share = lats // n_phys
 
-    outgoing = place_blocks(experts, cloudy_count, state, legendre.reshape(n_phys, share * CAP, coeffs // CAP))
+    outgoing = place_blocks(experts, cloudy_count, state, n_phys)
     arrived = lax.all_to_all(outgoing, "phys", split_axis=0, concat_axis=0, tiled=True)
 
     high, low = (jnp.asarray(part) for part in wave_table(waves, n_lon))
     chunk_waves = band_waves.reshape(n_dyn, n_phys).T.reshape(waves, 1)
     order = (chunk_waves == jnp.arange(waves, dtype=jnp.int32)[None, :]).astype(BF16)
-    table, first, gain, pull, regain, first_w, middle_w, last_w = prepare(
+    table, first, gain, pull, regain, shares, first_w, middle_w, last_w = prepare(
         state,
         prev,
         order,
@@ -519,20 +521,21 @@
         band_waves,
         analysis.reshape(levels, 2 * coeffs // LANES, LANES),
         nudge_rate[None, :],
-    )
-    arrived, first_w, middle_w, last_w, *kept = lax.optimization_barrier(
-        (arrived, first_w, middle_w, last_w, table, first, gain, pull, regain)
-    )
-    computed, own, table, first, gain, pull, regain = network(
-        arrived, first_w, middle_w, last_w, *kept
+        legendre.reshape(n_phys, share * CAP, coeffs // CAP),
+    )
+    arrived, first_w, middle_w, last_w, shares, *kept = lax.optimization_barrier(
+        (arrived, first_w, middle_w, last_w, shares, table, first, gain, pull, regain)
+    )
+    computed, table, first, gain, pull, regain = network(
+        arrived, first_w, middle_w, last_w, shares, *kept
     )
     returned = lax.all_to_all(computed, "phys", split_axis=0, concat_axis=0, tiled=True)
 
-    tendency, sent = return_blocks(returned, experts, cloudy_count, table, first)
+    tendency, sent = return_blocks(levels, returned, experts, cloudy_count, table, first)
     got = lax.all_to_all(
         sent.reshape(waves, 4, LANES), ORDER, split_axis=0, concat_axis=0, tiled=True
     )
-    back = solve_twice(got.reshape(4 * lats, LANES), own, gain, pull, regain)
+    back = solve_twice(share, got.reshape(4 * lats, LANES), returned, gain, pull, regain)
     home = lax.all_to_all(
         back.reshape(lats, 2, LANES), ORDER, split_axis=0, concat_axis=0, tiled=True
     )

time: 98.4 us -> 99 us (level)
  waiting for transfers between devices: 7.05 us -> 5.32 us
  blocking collectives: 63.7 us -> 65.2 us
  Pallas kernels: 17.5 us -> 18.5 us
    all_to_all x1, waiting for transfers between devices: 7.05 us -> 5.32 us  [on_device(): lax.all_to_all(outgoing, 'phys', split_axis=0, concat_axis=0, tiled=True)]
    all_to_all x1, blocking collectives: 26.5 us -> 27.8 us  [on_device(): lax.all_to_all(sent.reshape(waves, 4, LANES), ORDER, split_axis=0, concat...]
    pallas_call x1, Pallas kernels: 4.21 us -> 5.27 us  [network(): pl.pallas_call(functools.partial(network_kernel, len(kept)), in_specs=[VM...]
where the time goes in v6:
time: 99 us; the launch traced here: 98.7 us
  blocking collectives  65.2 us (66%)
  Pallas kernels  18.5 us (19%)
  starting transfers between devices  8.46 us (9%)
  waiting for transfers between devices  5.32 us (5%)
    all_to_all x1, blocking collectives, on_device(): lax.all_to_all(sent.reshape(waves, 4, LANES), ORDER, split_axis=0, concat...  27.8 us
    all_to_all x1, blocking collectives, on_device(): lax.all_to_all(computed, 'phys', split_axis=0, concat_axis=0, tiled=True)  19 us
    all_to_all x1, blocking collectives, on_device(): lax.all_to_all(back.reshape(lats, 2, LANES), ORDER, split_axis=0, concat_...  18.4 us
    all_to_all x1, starting transfers between devices, on_device(): lax.all_to_all(outgoing, 'phys', split_axis=0, concat_axis=0, tiled=True)  8.46 us
    pallas_call x1, Pallas kernels, prepare(): pl.pallas_call(functools.partial(prepare_kernel, n_lon), in_specs=[VMEM]...  6.32 us
    all_to_all x1, waiting for transfers between devices, on_device(): lax.all_to_all(outgoing, 'phys', split_axis=0, concat_axis=0, tiled=True)  5.32 us
    pallas_call x1, Pallas kernels, network(): pl.pallas_call(functools.partial(network_kernel, len(kept)), in_specs=[VM...  5.27 us
    pallas_call x1, Pallas kernels, place_blocks(): pl.pallas_call(place_kernel, in_specs=[HBM] * 3, out_specs=VMEM, out_shap...  2.36 us
  transfers between devices with their start and end apart: 1, of which 1 were waited for; matrix products, arithmetic and copies ran while one was open for 0% of the time, Pallas kernels for 6%

profile of v6, /device:TPU:1, one launch (start us, length us, event | category | flops | bytes accessed | tf_op | source)
XLA Modules:
  0.0 98.7 jit_solution(7633031652619293034)
XLA Ops:
  0.6 0.0 copy-start.2
  0.6 2.4 %place.1 = bf16[16,72,256]{2,1,0:T(8,128)(2,1)} custom-call(s32[16]{0:T(128)} %bitcast.20, s32[16]{0:T(128)} %cloudy_ref.1, f32[72,16,128]{2,1,0:T(8,128)} %bitcast.22), custom_call_target="tpu_custom_call" | custom-call | tf_op jit(solution)/shard_map/place/pallas_call | solution.py:103
  3.0 8.5 %all-to-all-start = ((bf16[16,72,256]{2,1,0:T(8,128)(2,1)}), bf16[16,72,256]{2,1,0:T(8,128)(2,1)S(1)}, u32[]{:S(2)}, u32[]{:S(2)}) async-start(bf16[16,72,256]{2,1,0:T(8,128)(2,1)} %place.1), calls=%async_computation | async-start | bytes 1179648 | tf_op jit(solution)/shard_map/all_to_all | solution.py:507
  11.5 0.0 copy-done.2
  11.5 0.1 reshape.40
  11.6 0.1 copy.17
  11.6 0.1 eq.15
  11.7 0.1 fusion.order_ref
  11.8 6.3 %prepare.1 = (bf16[512,2048]{1,0:T(8,128)(2,1)}, bf16[512,128]{1,0:T(8,128)(2,1)}, f32[256,256]{1,0:T(8,128)}, f32[256,256]{1,0:T(8,128)}, f32[1,256]{1,0:T(1,12...) custom-call(bf16[256,256]{1,0:T(8,128)(2,1)S(1)} %fusion.order_ref, ...), custom_call_target="tpu_custom_call" | custom-call | flops 2147483648 | bytes 12582912 | tf_op jit(solution)/shard_map/prepare/pallas_call | solution.py:204
  18.2 5.3 %all-to-all-done.x_ref = bf16[16,72,256]{2,1,0:T(8,128)(2,1)S(1)} async-done(((bf16[16,72,256]{2,1,0:T(8,128)(2,1)}), bf16[16,72,256]{2,1,0:T(8,128)(2,1)S(1)}, u32[]{:S(2)}, u32[]{:S(2)}) %all-to-all-start) | async-done | bytes 589856 | tf_op jit(solution)/shard_map/all_to_all | solution.py:507
  23.5 0.0 copy-start
  23.5 0.0 copy-start.1
  23.5 5.3 %network.1 = (bf16[16,88,256]{2,1,0:T(8,128)(2,1)S(1)}, bf16[512,2048]{1,0:T(8,128)(2,1)S(1)}, bf16[512,128]{1,0:T(8,128)(2,1)S(1)}, f32[256,256]{1,0:T(8,128)S(...) custom-call(bf16[16,72,256]{2,1,0:T(8,128)(2,1)S(1)} %all-to-all-done.x_ref, ...), custom_call_target="tpu_custom_call" | custom-call | flops 6442450944 | bytes 4194304 | tf_op jit(solution)/shard_map/network/pallas_call | solution.py:319
  28.8 19.0 %all_to_all.20.returned_ref.own_ref = bf16[16,88,256]{2,1,0:T(8,128)(2,1)S(1)} all-to-all(bf16[16,88,256]{2,1,0:T(8,128)(2,1)S(1)} %get-tuple-element.48), channel_id=1, replica_groups=mesh['dyn'=16,'phys'=16] {'phys'}, dimensions={0} | all-to-all | bytes 1441792 | tf_op jit(solution)/shard_map/all_to_all | solution.py:532
  47.8 0.0 copy-done
  47.8 0.0 copy-done.1
  47.8 2.1 %return.1 = (bf16[72,2048]{1,0:T(8,128)(2,1)}, bf16[1024,128]{1,0:T(8,128)(2,1)S(1)}) custom-call(bf16[16,88,256]{2,1,0:T(8,128)(2,1)S(1)} %all_to_all.20.returned_ref.own_ref, bf16[512,2048]{1,0:T(8,128)(2,1)S(1)} %get-tuple-element.49.table_ref, bf16[512,128]{1,0:T(8,128)(2,1)S(1)} %get-tuple-element.50.first_ref, s32[16]{0:T(128)S(1)} %bitcast.21, ...), custom_call_target="tpu_custom_call" | custom-call | tf_op jit(solution)/shard_map/return/pallas_call | solution.py:382
  49.9 27.8 %all_to_all.21 = bf16[256,4,128]{2,1,0:T(4,128)(2,1)S(1)} all-to-all(bf16[256,4,128]{2,1,0:T(4,128)(2,1)S(1)} %bitcast.19), channel_id=1, replica_groups=mesh['dyn'=16,'phys'=16] {'phys','dyn'}, dimensions={0} | all-to-all | bytes 524288 | tf_op jit(solution)/shard_map/all_to_all | solution.py:535
  77.7 1.1 %solve.1 = bf16[512,128]{1,0:T(8,128)(2,1)S(1)} custom-call(bf16[1024,128]{1,0:T(8,128)(2,1)S(1)} %bitcast.16, bf16[16,88,256]{2,1,0:T(8,128)(2,1)S(1)} %all_to_all.20.returned_ref.own_ref, f32[256,256]{1,0:T(8,128)S(1)} %get-tuple-element.52.gain_ref, f32[256,256]{1,0:T(8,128)S(1)} %get-tuple-element.53.pull_ref, f32[1,256]{1,0:T(1,128)S(1)} %get-tuple-element.54.regain_ref), custom_call_target="tpu_custom_call" | custom-call | tf_op jit(solution)/shard_map/solve/pallas_call | solution.py:430
  78.7 18.4 %all_to_all.22 = bf16[256,2,128]{2,1,0:T(2,128)(2,1)S(1)} all-to-all(bf16[256,2,128]{2,1,0:T(2,128)(2,1)S(1)} %bitcast.18), channel_id=1, replica_groups=mesh['dyn'=16,'phys'=16] {'phys','dyn'}, dimensions={0} | all-to-all | bytes 262144 | tf_op jit(solution)/shard_map/all_to_all | solution.py:539
  97.1 1.4 %synthesis.1 = f32[72,16,128]{2,1,0:T(8,128)} custom-call(bf16[512,128]{1,0:T(8,128)(2,1)S(1)} %bitcast.17, bf16[512,2048]{1,0:T(8,128)(2,1)S(1)} %get-tuple-element.49.table_ref), custom_call_target="tpu_custom_call" | custom-call | tf_op jit(solution)/shard_map/synthesis/pallas_call | solution.py:465
Async XLA Ops:
  0.6 10.8 %copy-start.2 = (s32[256]{0:T(256)S(1)}, s32[256]{0:T(256)}, u32[]{:S(2)}) copy-start(s32[256]{0:T(256)} %wave_hbm.1) | copy-start | bytes 3076
  3.0 20.5 %all-to-all-start = ((bf16[16,72,256]{2,1,0:T(8,128)(2,1)}), bf16[16,72,256]{2,1,0:T(8,128)(2,1)S(1)}, u32[]{:S(2)}, u32[]{:S(2)}) async-start(bf16[16,72,256]{2,1,0:T(8,128)(2,1)} %place.1), calls=%async_computation | async-start | bytes 1179648 | tf_op jit(solution)/shard_map/all_to_all | solution.py:507
  23.5 24.3 %copy-start = (s32[16,1]{0,1:T(1,128)S(1)}, s32[16,1]{0,1:T(1,128)}, u32[]{:S(2)}) copy-start(s32[16,1]{0,1:T(1,128)} %param.20) | copy-start | bytes 196
  23.5 24.3 %copy-start.1 = (s32[16]{0:T(128)S(1)}, s32[16]{0:T(128)}, u32[]{:S(2)}) copy-start(s32[16]{0:T(128)} %cloudy_ref.1) | copy-start | bytes 196
